TPU v7x, 32 devices: a whole 2x2x4 slice. The times are simulated.
32 devices in a mesh: ctx: 8 (over y, x, core), fsdp: 4 (over z).
Axes of the slice: x: 2, y: 2, z: 4, core: 2. Of those that a mesh axis runs over, the one named last changes fastest.
Arguments:
- activations: bfloat16 [4, 8192, 1088], P('fsdp', 'ctx'), may hold values from -6 to 6
- doc_lengths: int32 [4, 6], P('fsdp'), may hold values from 1 to 8187, as said below
- cotangent: bfloat16 [4, 8192, 1088], P('fsdp', 'ctx'), may hold values from -6 to 6
- attn_gain: float32 [1088], P('fsdp'), may hold values from 0.5 to 1.5
- attn_shift: float32 [1088], P('fsdp'), may hold values from -1.75 to 1.75
- w_qkv: float32 [1088, 3264], P('fsdp'), may hold values from -0.1875 to 0.1875
- query_bias: float32 [1088], P('fsdp'), may hold values from -3 to 3
- value_bias: float32 [1088], P('fsdp'), may hold values from -3 to 3
- w_out: float32 [1088, 1088], P('fsdp'), may hold values from -0.75 to 0.75
- out_bias: float32 [1088], P('fsdp'), may hold values from -1.75 to 1.75
- mlp_gain: float32 [1088], P('fsdp'), may hold values from 0.5 to 1.5
- mlp_shift: float32 [1088], P('fsdp'), may hold values from -1.75 to 1.75
- w_fc: float32 [1088, 4352], P('fsdp'), may hold values from -0.1875 to 0.1875
- fc_bias: float32 [4352], P('fsdp'), may hold values from -1.75 to 1.75
- w_proj: float32 [4352, 1088], P('fsdp'), may hold values from -0.09375 to 0.09375
- proj_bias: float32 [1088], P('fsdp'), may hold values from -1.75 to 1.75
Outputs:
- block_out: bfloat16 [4, 8192, 1088], P('fsdp', 'ctx')
- input_grad: float32 [4, 8192, 1088], P('fsdp', 'ctx')
- attn_gain_grad: float32 [1088], P('fsdp')
- attn_shift_grad: float32 [1088], P('fsdp')
- w_qkv_grad: float32 [1088, 3264], P('fsdp')
- query_bias_grad: float32 [1088], P('fsdp')
- value_bias_grad: float32 [1088], P('fsdp')
- w_out_grad: float32 [1088, 1088], P('fsdp')
- out_bias_grad: float32 [1088], P('fsdp')
- mlp_gain_grad: float32 [1088], P('fsdp')
- mlp_shift_grad: float32 [1088], P('fsdp')
- w_fc_grad: float32 [1088, 4352], P('fsdp')
- fc_bias_grad: float32 [4352], P('fsdp')
- w_proj_grad: float32 [4352, 1088], P('fsdp')
- proj_bias_grad: float32 [1088], P('fsdp')
Inputs may be any that keep to these rules, and one draw needn't show every extreme that they name: `doc_lengths`: in each sequence the 6 lengths are positive and sum to 8192; one of them is longer than 7168.
All inputs are finite; a program needn't handle non-finite values.
Results may differ from a plain program's by a relative error of at most 0.014.
The roundings to bfloat16 on the way count: a program that leaves them out, or rounds other values in their place, can miss the bound.
Values may be sent and summed in bfloat16 or wider, within the bound.
A program may use at most 448 MiB of HBM per device.

v0:
```python
import math

import jax
import jax.numpy as jnp
from jax import lax
from jax.sharding import PartitionSpec as P

HEAD = 64
WINDOW = 1024


epsilon = 1e-05
masked_score = -1e30


def passed_along(value, axis, by):
    peers = lax.axis_size(axis)
    pairs = [(i, i + by) for i in range(peers) if 0 <= i + by < peers]
    return lax.ppermute(value, axis, pairs)


def layer_norm(values, gain, shift):
    middle = jnp.mean(values, axis=-1, keepdims=True)
    centred = values - middle
    spread = jnp.mean(centred * centred, axis=-1, keepdims=True)
    return centred * lax.rsqrt(spread + epsilon) * gain + shift


def gelu_tanh(values):
    return jax.nn.gelu(values, approximate=True)


def segment_ids(lengths_row, positions):
    ends = jnp.cumsum(lengths_row)
    found = jnp.sum((positions[:, None] >= ends[None, :]).astype(jnp.int32), axis=1)
    return jnp.where(positions >= 0, found, -1)


def gather_first(masters):
    lows = [item.astype(jnp.bfloat16) for item in masters]
    return (
        lax.all_gather(lows[0], "fsdp", axis=0, tiled=True),
        lax.all_gather(lows[1], "fsdp", axis=0, tiled=True),
        lax.all_gather(lows[2], "fsdp", axis=0, tiled=True),
        lax.all_gather(lows[3], "fsdp", axis=0, tiled=True),
        lax.all_gather(lows[4], "fsdp", axis=0, tiled=True),
        lax.all_gather(lows[5], "fsdp", axis=0, tiled=True),
        lax.all_gather(lows[6], "fsdp", axis=0, tiled=True),
        lax.all_gather(lows[7], "fsdp", axis=0, tiled=True),
        lax.all_gather(lows[8], "fsdp", axis=0, tiled=True),
        lax.all_gather(lows[9], "fsdp", axis=0, tiled=True),
        lax.all_gather(lows[10], "fsdp", axis=0, tiled=True),
        lax.all_gather(lows[11], "fsdp", axis=0, tiled=True),
        lax.all_gather(lows[12], "fsdp", axis=0, tiled=True),
    )


def gather_second(masters):
    lows = [item.astype(jnp.bfloat16) for item in masters]
    return (
        lax.all_gather(lows[0], "fsdp", axis=0, tiled=True),
        lax.all_gather(lows[1], "fsdp", axis=0, tiled=True),
        lax.all_gather(lows[2], "fsdp", axis=0, tiled=True),
        lax.all_gather(lows[3], "fsdp", axis=0, tiled=True),
        lax.all_gather(lows[4], "fsdp", axis=0, tiled=True),
        lax.all_gather(lows[5], "fsdp", axis=0, tiled=True),
        lax.all_gather(lows[6], "fsdp", axis=0, tiled=True),
        lax.all_gather(lows[7], "fsdp", axis=0, tiled=True),
        lax.all_gather(lows[8], "fsdp", axis=0, tiled=True),
        lax.all_gather(lows[9], "fsdp", axis=0, tiled=True),
        lax.all_gather(lows[10], "fsdp", axis=0, tiled=True),
        lax.all_gather(lows[11], "fsdp", axis=0, tiled=True),
        lax.all_gather(lows[12], "fsdp", axis=0, tiled=True),
    )


def on_device(
    activations,
    doc_lengths,
    cotangent,
    attn_gain,
    attn_shift,
    w_qkv,
    query_bias,
    value_bias,
    w_out,
    out_bias,
    mlp_gain,
    mlp_shift,
    w_fc,
    fc_bias,
    w_proj,
    proj_bias,
):
    masters = (
        attn_gain,
        attn_shift,
        w_qkv,
        query_bias,
        value_bias,
        w_out,
        out_bias,
        mlp_gain,
        mlp_shift,
        w_fc,
        fc_bias,
        w_proj,
        proj_bias,
    )
    weights = gather_first(masters)
    gain_one, shift_one, qkv_low, qbias_low, vbias_low, out_low, obias_low = weights[:7]
    gain_two, shift_two, fc_low, fcbias_low, proj_low, pbias_low = weights[7:]
    tokens = activations[0].astype(jnp.float32)
    tok_rows = tokens.shape[0]
    features = tokens.shape[1]
    head_count = features // HEAD
    score_scale = 1.0 / math.sqrt(HEAD)
    normed1, norm1_back = jax.vjp(
        layer_norm, tokens, gain_one.astype(jnp.float32), shift_one.astype(jnp.float32)
    )
    normed1_low = normed1.astype(jnp.bfloat16)
    bias_all = jnp.concatenate([qbias_low, jnp.zeros_like(qbias_low), vbias_low]).astype(
        jnp.float32
    )
    qkv = (jnp.dot(normed1_low, qkv_low, preferred_element_type=jnp.float32) + bias_all).astype(
        jnp.bfloat16
    )
    queries = qkv[:, :features].reshape(tok_rows, head_count, HEAD)
    keys = qkv[:, features : 2 * features].reshape(tok_rows, head_count, HEAD)
    values = qkv[:, 2 * features :].reshape(tok_rows, head_count, HEAD)
    tails = jnp.stack([keys, values])
    earlier = passed_along(tails, "ctx", 1)
    keys_ext = jnp.concatenate([earlier[0], keys], axis=0)
    values_ext = jnp.concatenate([earlier[1], values], axis=0)
    first_pos = lax.axis_index("ctx") * tok_rows
    positions = first_pos + jnp.arange(tok_rows, dtype=jnp.int32)
    ext_positions = first_pos - WINDOW + jnp.arange(tok_rows + WINDOW, dtype=jnp.int32)
    doc_rows = segment_ids(doc_lengths[0], positions)
    doc_ext = segment_ids(doc_lengths[0], ext_positions)
    block_rows = min(512, tok_rows)
    block_count = tok_rows // block_rows
    key_span = block_rows + WINDOW

    def block_scores(index):
        start = index * block_rows
        query_pos = lax.dynamic_slice_in_dim(positions, start, block_rows, 0)
        key_pos = lax.dynamic_slice_in_dim(ext_positions, start, key_span, 0)
        distance = query_pos[:, None] - key_pos[None, :]
        same_doc = (
            lax.dynamic_slice_in_dim(doc_rows, start, block_rows, 0)[:, None]
            == lax.dynamic_slice_in_dim(doc_ext, start, key_span, 0)[None, :]
        )
        allowed = (distance >= 0) & (distance <= WINDOW) & same_doc
        query_block = lax.dynamic_slice_in_dim(queries, start, block_rows, 0)
        key_block = lax.dynamic_slice_in_dim(keys_ext, start, key_span, 0)
        value_block = lax.dynamic_slice_in_dim(values_ext, start, key_span, 0)
        scores = (
            jnp.einsum("qhe,khe->hqk", query_block, key_block, preferred_element_type=jnp.float32)
            * score_scale
        )
        return (
            start,
            query_block,
            key_block,
            value_block,
            jnp.where(allowed[None], scores, masked_score),
        )

    def forward_block(index):
        start, query_block, key_block, value_block, scores = block_scores(index)
        row_max = jnp.max(scores, axis=-1, keepdims=True)
        expo = jnp.exp(scores - row_max)
        row_total = jnp.sum(expo, axis=-1, keepdims=True)
        probability = (expo / row_total).astype(jnp.bfloat16)
        mixed = jnp.einsum(
            "hqk,khe->qhe", probability, value_block, preferred_element_type=jnp.float32
        )
        return (mixed.reshape(block_rows, features), (row_max + jnp.log(row_total))[..., 0])

    mixed_blocks, log_totals = lax.map(forward_block, jnp.arange(block_count, dtype=jnp.int32))
    attended_low = mixed_blocks.reshape(tok_rows, features).astype(jnp.bfloat16)
    resid = (
        tokens
        + jnp.dot(attended_low, out_low, preferred_element_type=jnp.float32)
        + obias_low.astype(jnp.float32)
    )
    normed2, norm2_back = jax.vjp(
        layer_norm, resid, gain_two.astype(jnp.float32), shift_two.astype(jnp.float32)
    )
    normed2_low = normed2.astype(jnp.bfloat16)
    pre_act = jnp.dot(normed2_low, fc_low, preferred_element_type=jnp.float32) + fcbias_low.astype(
        jnp.float32
    )
    activated, gelu_back = jax.vjp(gelu_tanh, pre_act)
    activated_low = activated.astype(jnp.bfloat16)
    final = (
        resid
        + jnp.dot(activated_low, proj_low, preferred_element_type=jnp.float32)
        + pbias_low.astype(jnp.float32)
    )
    block_out = final.astype(jnp.bfloat16)[None]
    back_weights = gather_second(masters)
    qkv_back = back_weights[2]
    out_back = back_weights[5]
    fc_back = back_weights[9]
    proj_back = back_weights[11]
    grad_final = cotangent[0]
    grad_final32 = grad_final.astype(jnp.float32)
    grad_wproj = jnp.einsum(
        "tf,td->fd", activated_low, grad_final, preferred_element_type=jnp.float32
    )
    grad_pbias = jnp.sum(grad_final32, axis=0)
    grad_act = jnp.einsum("td,fd->tf", grad_final, proj_back, preferred_element_type=jnp.float32)
    grad_pre = gelu_back(grad_act)[0].astype(jnp.bfloat16)
    grad_wfc = jnp.einsum("td,tf->df", normed2_low, grad_pre, preferred_element_type=jnp.float32)
    grad_fcbias = jnp.sum(grad_pre.astype(jnp.float32), axis=0)
    grad_normed2 = jnp.einsum("tf,df->td", grad_pre, fc_back, preferred_element_type=jnp.float32)
    grad_resid_norm, grad_gain_two, grad_shift_two = norm2_back(grad_normed2)
    grad_resid = grad_final32 + grad_resid_norm
    grad_branch = grad_resid.astype(jnp.bfloat16)
    grad_wout = jnp.einsum(
        "td,te->de", attended_low, grad_branch, preferred_element_type=jnp.float32
    )
    grad_obias = jnp.sum(grad_branch.astype(jnp.float32), axis=0)
    grad_attended = jnp.einsum(
        "te,de->td", grad_branch, out_back, preferred_element_type=jnp.float32
    ).astype(jnp.bfloat16)
    grad_att_heads = grad_attended.reshape(tok_rows, head_count, HEAD)

    def backward_block(carry, index):
        ext_grad_key, ext_grad_value = carry
        start, query_block, key_block, value_block, scores = block_scores(index)
        probability = jnp.exp(scores - log_totals[index][..., None])
        grad_out_block = lax.dynamic_slice_in_dim(grad_att_heads, start, block_rows, 0)
        grad_prob = jnp.einsum(
            "qhe,khe->hqk", grad_out_block, value_block, preferred_element_type=jnp.float32
        )
        inner = jnp.sum(probability * grad_prob, axis=-1, keepdims=True)
        grad_scores = (probability * (grad_prob - inner)).astype(jnp.bfloat16)
        grad_query = (
            jnp.einsum("hqk,khe->qhe", grad_scores, key_block, preferred_element_type=jnp.float32)
            * score_scale
        )
        grad_key = (
            jnp.einsum("hqk,qhe->khe", grad_scores, query_block, preferred_element_type=jnp.float32)
            * score_scale
        )
        grad_value = jnp.einsum(
            "hqk,qhe->khe",
            probability.astype(jnp.bfloat16),
            grad_out_block,
            preferred_element_type=jnp.float32,
        )
        ext_grad_key = lax.dynamic_update_slice_in_dim(
            ext_grad_key,
            lax.dynamic_slice_in_dim(ext_grad_key, start, key_span, 0) + grad_key,
            start,
            0,
        )
        ext_grad_value = lax.dynamic_update_slice_in_dim(
            ext_grad_value,
            lax.dynamic_slice_in_dim(ext_grad_value, start, key_span, 0) + grad_value,
            start,
            0,
        )
        return ((ext_grad_key, ext_grad_value), grad_query)

    empty = jnp.zeros((tok_rows + WINDOW, head_count, HEAD), jnp.float32)
    (ext_grad_key, ext_grad_value), grad_queries = lax.scan(
        backward_block, (empty, empty), jnp.arange(block_count, dtype=jnp.int32)
    )
    returned = passed_along(
        jnp.stack([ext_grad_key[:WINDOW], ext_grad_value[:WINDOW]]).astype(jnp.bfloat16), "ctx", -1
    ).astype(jnp.float32)
    grad_keys = ext_grad_key[WINDOW:].at[tok_rows - WINDOW :].add(returned[0])
    grad_values = ext_grad_value[WINDOW:].at[tok_rows - WINDOW :].add(returned[1])
    grad_qkv = jnp.concatenate(
        [
            grad_queries.reshape(tok_rows, features),
            grad_keys.reshape(tok_rows, features),
            grad_values.reshape(tok_rows, features),
        ],
        axis=1,
    ).astype(jnp.bfloat16)
    grad_wqkv = jnp.einsum("td,te->de", normed1_low, grad_qkv, preferred_element_type=jnp.float32)
    column_sums = jnp.sum(grad_qkv.astype(jnp.float32), axis=0)
    grad_qbias = column_sums[:features]
    grad_vbias = column_sums[2 * features :]
    grad_normed1 = jnp.einsum("te,de->td", grad_qkv, qkv_back, preferred_element_type=jnp.float32)
    grad_tokens_norm, grad_gain_one, grad_shift_one = norm1_back(grad_normed1)
    input_grad = (grad_resid + grad_tokens_norm)[None]
    matrices = (
        lax.psum_scatter(
            grad_wqkv.astype(jnp.bfloat16), "ctx", scatter_dimension=1, tiled=True
        ).astype(jnp.float32),
        lax.psum_scatter(
            grad_wout.astype(jnp.bfloat16), "ctx", scatter_dimension=1, tiled=True
        ).astype(jnp.float32),
        lax.psum_scatter(
            grad_wfc.astype(jnp.bfloat16), "ctx", scatter_dimension=1, tiled=True
        ).astype(jnp.float32),
        lax.psum_scatter(
            grad_wproj.astype(jnp.bfloat16), "ctx", scatter_dimension=1, tiled=True
        ).astype(jnp.float32),
    )
    shards = (
        lax.psum_scatter(grad_gain_one, "fsdp", scatter_dimension=0, tiled=True),
        lax.psum_scatter(grad_shift_one, "fsdp", scatter_dimension=0, tiled=True),
        lax.psum_scatter(matrices[0], "fsdp", scatter_dimension=0, tiled=True),
        lax.psum_scatter(grad_qbias, "fsdp", scatter_dimension=0, tiled=True),
        lax.psum_scatter(grad_vbias, "fsdp", scatter_dimension=0, tiled=True),
        lax.psum_scatter(matrices[1], "fsdp", scatter_dimension=0, tiled=True),
        lax.psum_scatter(grad_obias, "fsdp", scatter_dimension=0, tiled=True),
        lax.psum_scatter(grad_gain_two, "fsdp", scatter_dimension=0, tiled=True),
        lax.psum_scatter(grad_shift_two, "fsdp", scatter_dimension=0, tiled=True),
        lax.psum_scatter(matrices[2], "fsdp", scatter_dimension=0, tiled=True),
        lax.psum_scatter(grad_fcbias, "fsdp", scatter_dimension=0, tiled=True),
        lax.psum_scatter(matrices[3], "fsdp", scatter_dimension=0, tiled=True),
        lax.psum_scatter(grad_pbias, "fsdp", scatter_dimension=0, tiled=True),
    )
    joined = (
        lax.all_gather(shards[2].astype(jnp.bfloat16), "ctx", axis=1, tiled=True).astype(
            jnp.float32
        ),
        lax.all_gather(shards[5].astype(jnp.bfloat16), "ctx", axis=1, tiled=True).astype(
            jnp.float32
        ),
        lax.all_gather(shards[9].astype(jnp.bfloat16), "ctx", axis=1, tiled=True).astype(
            jnp.float32
        ),
        lax.all_gather(shards[11].astype(jnp.bfloat16), "ctx", axis=1, tiled=True).astype(
            jnp.float32
        ),
    )
    vectors = lax.psum(
        (
            shards[0],
            shards[1],
            shards[3],
            shards[4],
            shards[6],
            shards[7],
            shards[8],
            shards[10],
            shards[12],
        ),
        "ctx",
    )
    summed = (
        vectors[0],
        vectors[1],
        joined[0],
        vectors[2],
        vectors[3],
        joined[1],
        vectors[4],
        vectors[5],
        vectors[6],
        joined[2],
        vectors[7],
        joined[3],
        vectors[8],
    )
    return (
        block_out,
        input_grad,
        summed[0],
        summed[1],
        summed[2],
        summed[3],
        summed[4],
        summed[5],
        summed[6],
        summed[7],
        summed[8],
        summed[9],
        summed[10],
        summed[11],
        summed[12],
    )


def solution(mesh):
    placed = (
        P("fsdp", "ctx", None),
        P("fsdp", None),
        P("fsdp", "ctx", None),
        P("fsdp"),
        P("fsdp"),
        P("fsdp", None),
        P("fsdp"),
        P("fsdp"),
        P("fsdp", None),
        P("fsdp"),
        P("fsdp"),
        P("fsdp"),
        P("fsdp", None),
        P("fsdp"),
        P("fsdp", None),
        P("fsdp"),
    )
    return jax.shard_map(
        on_device,
        mesh=mesh,
        in_specs=placed,
        out_specs=(
            P("fsdp", "ctx", None),
            P("fsdp", "ctx", None),
            P("fsdp"),
            P("fsdp"),
            P("fsdp", None),
            P("fsdp"),
            P("fsdp"),
            P("fsdp", None),
            P("fsdp"),
            P("fsdp"),
            P("fsdp"),
            P("fsdp", None),
            P("fsdp"),
            P("fsdp", None),
            P("fsdp"),
        ),
        check_vma=False,
    )
```

profile of v0, /device:TPU:7, one launch (start us, length us, event | category | flops | bytes accessed | tf_op | source)
XLA Modules:
  0.0 1642.1 jit_solution(9689869481530187172)
XLA Ops:
  43.6 101.1 %all-gather.10.cloned.1.call-done = bf16[1088,3264]{1,0:T(8,128)(2,1)} async-done(((bf16[272,3264]{1,0:T(8,128)(2,1)}), bf16[1088,3264]{1,0:T(8,128)(2,1)}) %all-gather.10.cloned.1.call-update) | async-done | bytes 7102480 | tf_op jit(solution)/shard_map/all_gather | solution.py:44
  178.2 146.5 %while.30 = (s32[]{:T(128)}, bf16[2,512,1088]{1,2,0:T(8,128)(2,1)}, f32[2,17,512]{2,1,0:T(8,128)S(1)}, s32[2]{0:T(128)S(1)}, bf16[2048,17,64]{0,2,1:T(8,128)(2,1...) while((s32[]{:T(128)}, bf16[2,512,1088]{1,2,0:T(8,128)(2,1)}, ...), condition=%wide.region_8.9_spmd, body=%wide.region_5.8_spmd.sunk | while | flops 3587694080 | bytes 175089936 | solution.py:180
  201.8 24.3 %fusion.128 = f32[17,512]{1,0:T(8,128)S(1)} fusion(f32[17,512,1536]{2,1,0:T(8,128)} %get-tuple-element.522, f32[17,512]{1,0:T(8,128)S(1)} %get-tuple-element.523, pred[512,1536]{1,0:T(8,128)(4,1)S(1)} %fusion.126), kind=kLoop, calls=%fused_computation.4.clone.1 | loop fusion | flops 53468672 | bytes 54333440 | tf_op jit(solution)/shard_map/while/body/eval_jaxpr/reduce_sum | solution.py:173
  226.1 23.7 %fusion.129 = bf16[17,64,512]{2,1,0:T(8,128)(2,1)} fusion(f32[17,512,1536]{2,1,0:T(8,128)} %get-tuple-element.522, f32[17,512]{1,0:T(8,128)S(1)} %fusion.128, f32[17,512]{1,0:T(8,128)S(1)} %get-tuple-element.523, pred[512,1536]{1,0:T(8,128)(4,1)S(1)} %fusion.126, bf16[2048,17,64]{0,2,1:T(8,128)(2,1)} %get-tuple-element.576, s32[]{:T(128)S(6)} %select_n.85), kind=kOutput, calls=%fused_computation.5.clone.1 | convolution fusion | flops 1778122752 | bytes 58789892 | tf_op jit(solution)/shard_map/while/body/eval_jaxpr/hqk,khe->qhe/dot_general | solution.py:175
  298.8 23.5 %fusion.129 = bf16[17,64,512]{2,1,0:T(8,128)(2,1)} fusion(f32[17,512,1536]{2,1,0:T(8,128)} %get-tuple-element.522, f32[17,512]{1,0:T(8,128)S(1)} %fusion.128, f32[17,512]{1,0:T(8,128)S(1)} %get-tuple-element.523, pred[512,1536]{1,0:T(8,128)(4,1)S(1)} %fusion.126, bf16[2048,17,64]{0,2,1:T(8,128)(2,1)} %get-tuple-element.576, s32[]{:T(128)S(6)} %select_n.85), kind=kOutput, calls=%fused_computation.5.clone.1 | convolution fusion | flops 1778122752 | bytes 58789892 | tf_op jit(solution)/shard_map/while/body/eval_jaxpr/hqk,khe->qhe/dot_general | solution.py:175
  338.7 26.6 %all-gather.14.cloned.1.call-done = bf16[1088,4352]{1,0:T(8,128)(2,1)} async-done(((bf16[272,4352]{1,0:T(8,128)(2,1)}), bf16[1088,4352]{1,0:T(8,128)(2,1)}) %all-gather.14.cloned.1.call-update) | async-done | bytes 9469968 | tf_op jit(solution)/shard_map/all_gather | solution.py:51
  385.5 156.4 %all-gather.16.cloned.1.call-done = bf16[4352,1088]{1,0:T(8,128)(2,1)} async-done(((bf16[1088,1088]{1,0:T(8,128)(2,1)}), bf16[4352,1088]{1,0:T(8,128)(2,1)}) %all-gather.16.cloned.1.call-update) | async-done | bytes 9469968 | tf_op jit(solution)/shard_map/all_gather | solution.py:53
  541.9 28.4 %convert_reduce_fusion = (f32[4352]{0:T(1024)}, bf16[1024,4352]{1,0:T(8,128)(2,1)}) fusion(f32[1024,4352]{1,0:T(8,128)} %fusion.84, f32[4352]{0:T(1024)S(1)} %copy-done.43, bf16[4352,1088]{1,0:T(8,128)(2,1)} %all-gather.16.cloned.1.call-done, bf16[1,1024,1088]{1,2,0:T(8,128)(2,1)} %param.30), kind=kOutput, calls=%fused_computation.64 | convolution fusion | flops 9799725056 | bytes 38471680 | tf_op jit(solution)/shard_map/td,fd->tf/dot_general | solution.py:213
  607.6 342.3 %while.31 = (s32[]{:T(128)}, f32[2048,17,64]{0,2,1:T(8,128)}, f32[2048,17,64]{0,2,1:T(8,128)}, bf16[2,512,17,64]{1,3,2,0:T(8,128)(2,1)}, s32[2]{0:T(128)S(1)}, /...) while((s32[]{:T(128)}, f32[2048,17,64]{0,2,1:T(8,128)}, ...), condition=%wide.region_15.16_spmd, body=%wide.region_13.15_spmd.sunk | while | flops 8767201280 | bytes 457650976 | solution.py:269
  635.2 27.0 %fusion.141 = f32[2048,17,64]{0,2,1:T(8,128)} fusion(f32[2048,17,64]{0,2,1:T(8,128)} %get-tuple-element.610, s32[]{:T(128)S(6)} %select_n.90, f32[17,512,1536]{2,1,0:T(8,128)} %fusion.138, f32[17,512]{1,0:T(8,128)S(1)} %dynamic-slice_bitcast_fusion.2, pred[512,1536]{1,0:T(8,128)(4,1)S(1)} %fusion.139, bf16[1024,17,64]{0,2,1:T(8,128)(2,1)} %get-tuple-element.640, ...), kind=kOutput, calls=%fused_computation.27.clone.1 | convolution fusion | flops 1766424576 | bytes 68782088 | tf_op jit(solution)/shard_map/while/body/eval_jaxpr/hqk,qhe->khe/dot_general | solution.py:248
  662.2 41.6 %multiply_reduce_fusion.5 = (f32[17,512]{1,0:T(8,128)S(1)}, f32[17,512,1536]{2,1,0:T(8,128)}) fusion(f32[17,512,1536]{2,1,0:T(8,128)} %fusion.138, f32[17,512]{1,0:T(8,128)S(1)} %dynamic-slice_bitcast_fusion.2, pred[512,1536]{1,0:T(8,128)(4,1)S(1)} %fusion.139, bf16[2048,17,64]{0,2,1:T(8,128)(2,1)} %get-tuple-element.641, s32[]{:T(128)S(6)} %select_n.90, ...), kind=kOutput, calls=%fused_computation.21.clone.3 | convolution fusion | flops 1778114048 | bytes 112281608 | tf_op jit(solution)/shard_map/while/body/eval_jaxpr/qhe,khe->hqk/dot_general | solution.py:235
  703.7 42.2 %multiply_convert_fusion.5 = bf16[17,512,1536]{2,1,0:T(8,128)(2,1)} fusion(f32[17,512,1536]{2,1,0:T(8,128)} %get-tuple-element.538, f32[17,512,1536]{2,1,0:T(8,128)} %fusion.138, f32[17,512]{1,0:T(8,128)S(1)} %get-tuple-element.539, f32[17,512]{1,0:T(8,128)S(1)} %dynamic-slice_bitcast_fusion.2, pred[512,1536]{1,0:T(8,128)(4,1)S(1)} %fusion.139), kind=kLoop, calls=%fused_computation.20.clone.1 | loop fusion | flops 80216064 | bytes 134549504 | tf_op jit(solution)/shard_map/while/body/eval_jaxpr/convert_element_type | solution.py:239
  806.0 27.1 %fusion.141 = f32[2048,17,64]{0,2,1:T(8,128)} fusion(f32[2048,17,64]{0,2,1:T(8,128)} %get-tuple-element.610, s32[]{:T(128)S(6)} %select_n.90, f32[17,512,1536]{2,1,0:T(8,128)} %fusion.138, f32[17,512]{1,0:T(8,128)S(1)} %dynamic-slice_bitcast_fusion.2, pred[512,1536]{1,0:T(8,128)(4,1)S(1)} %fusion.139, bf16[1024,17,64]{0,2,1:T(8,128)(2,1)} %get-tuple-element.640, ...), kind=kOutput, calls=%fused_computation.27.clone.1 | convolution fusion | flops 1766424576 | bytes 68782088 | tf_op jit(solution)/shard_map/while/body/eval_jaxpr/hqk,qhe->khe/dot_general | solution.py:248
  833.0 41.6 %multiply_reduce_fusion.5 = (f32[17,512]{1,0:T(8,128)S(1)}, f32[17,512,1536]{2,1,0:T(8,128)}) fusion(f32[17,512,1536]{2,1,0:T(8,128)} %fusion.138, f32[17,512]{1,0:T(8,128)S(1)} %dynamic-slice_bitcast_fusion.2, pred[512,1536]{1,0:T(8,128)(4,1)S(1)} %fusion.139, bf16[2048,17,64]{0,2,1:T(8,128)(2,1)} %get-tuple-element.641, s32[]{:T(128)S(6)} %select_n.90, ...), kind=kOutput, calls=%fused_computation.21.clone.3 | convolution fusion | flops 1778114048 | bytes 112281608 | tf_op jit(solution)/shard_map/while/body/eval_jaxpr/qhe,khe->hqk/dot_general | solution.py:235
  874.6 42.2 %multiply_convert_fusion.5 = bf16[17,512,1536]{2,1,0:T(8,128)(2,1)} fusion(f32[17,512,1536]{2,1,0:T(8,128)} %get-tuple-element.538, f32[17,512,1536]{2,1,0:T(8,128)} %fusion.138, f32[17,512]{1,0:T(8,128)S(1)} %get-tuple-element.539, f32[17,512]{1,0:T(8,128)S(1)} %dynamic-slice_bitcast_fusion.2, pred[512,1536]{1,0:T(8,128)(4,1)S(1)} %fusion.139), kind=kLoop, calls=%fused_computation.20.clone.1 | loop fusion | flops 80216064 | bytes 134549504 | tf_op jit(solution)/shard_map/while/body/eval_jaxpr/convert_element_type | solution.py:239
  1033.0 63.7 %reduce-scatter.33.cloned.1.call-done = bf16[1088,408]{0,1:T(8,128)(2,1)} async-done(((bf16[1088,3264]{0,1:T(8,128)(2,1)}), bf16[1088,408]{0,1:T(8,128)(2,1)}) %reduce-scatter.33.cloned.1.call-update) | async-done | bytes 887824
  1099.4 80.0 %reduce-scatter.21.cloned.1.call-done = bf16[1088,544]{0,1:T(8,128)(2,1)} async-done(((bf16[1088,4352]{0,1:T(8,128)(2,1)}), bf16[1088,544]{0,1:T(8,128)(2,1)}) %reduce-scatter.21.cloned.1.call-update) | async-done | bytes 1183760 | tf_op jit(solution)/shard_map/reduce_scatter | solution.py:299
  1182.4 81.7 %reduce-scatter.23.cloned.1.call-done = bf16[4352,136]{0,1:T(8,128)(2,1)} async-done(((bf16[4352,1088]{0,1:T(8,128)(2,1)}), bf16[4352,136]{0,1:T(8,128)(2,1)}) %reduce-scatter.23.cloned.1.call-update) | async-done | bytes 1183760 | tf_op jit(solution)/shard_map/reduce_scatter | solution.py:302
  1268.1 43.6 %reduce-scatter.35.cloned.1.call-done = bf16[1088,136]{0,1:T(8,128)(2,1)} async-done(((bf16[1088,1088]{0,1:T(8,128)(2,1)}), bf16[1088,136]{0,1:T(8,128)(2,1)}) %reduce-scatter.35.cloned.1.call-update) | async-done | bytes 295952
  1313.9 47.5 %reduce-scatter.25.cloned.1.call-done = f32[272,408]{1,0:T(8,128)} async-done(((f32[1088,408]{1,0:T(8,128)}), f32[272,408]{1,0:T(8,128)}) %reduce-scatter.25.cloned.1.call-update) | async-done | bytes 443920
  1363.7 54.7 %reduce-scatter.29.cloned.1.call-done = f32[272,544]{1,0:T(8,128)} async-done(((f32[1088,544]{1,0:T(8,128)}), f32[272,544]{1,0:T(8,128)}) %reduce-scatter.29.cloned.1.call-update) | async-done | bytes 591888
  1422.0 24.0 %fusion.69 = bf16[1,1024,1088]{1,2,0:T(8,128)(2,1)} fusion(f32[1024,1088]{0,1:T(8,128)} %copy-done.7, bf16[4352,1088]{1,0:T(8,128)(2,1)} %all-gather.16.cloned.1.call-done, f32[1088]{0:T(1024)S(1)} %convert_element_type.217, f32[1024,4352]{1,0:T(8,128)} %fusion.84, f32[4352]{0:T(1024)S(1)} %copy-done.44), kind=kOutput, calls=%fused_computation.113 | convolution fusion | flops 9745137664 | bytes 34002176 | tf_op jit(solution)/shard_map/dot_general | solution.py:198
  1446.0 56.3 %reduce-scatter.31.cloned.1.call-done = f32[1088,136]{1,0:T(8,128)} async-done(((f32[4352,136]{1,0:T(8,128)}), f32[1088,136]{1,0:T(8,128)}) %reduce-scatter.31.cloned.1.call-update) | async-done | bytes 591888
  1545.0 24.6 %all-reduce.20 = (f32[272]{0:T(512)}, f32[272]{0:T(512)}, f32[272]{0:T(512)}, f32[272]{0:T(512)}, f32[272]{0:T(512)}, /*index=5*/f32[272]{0:T(512)}, f32[272]{0:T(512)}, f32[1088]{0:T(1024)}, f32[272]{0:T(512)}) all-reduce(f32[272]{0:T(512)S(1)} %dynamic-slice.20, ...), channel_id=1, replica_groups=mesh['ctx'=8,'fsdp'=4] {'ctx'}, use_global_device_ids=true, to_apply=%region_20.21 | all-reduce | flops 3264 | bytes 26112 | tf_op jit(solution)/shard_map/psum | solution.py:335
  (381 shorter events, 535.1 us)
Async XLA Ops:
  7.2 137.5 %all-gather.10.cloned.1.call-start = ((), (), s32[]{:S(2)}) async-start(), calls=%async_computation.8 | async-start | bytes 9052160 | tf_op jit(solution)/shard_map/all_gather | solution.py:44
  10.8 318.6 %all-gather.12.cloned.1.call-start = ((), (), s32[]{:S(2)}) async-start(), calls=%async_computation.9 | async-start | bytes 3133440 | tf_op jit(solution)/shard_map/all_gather | solution.py:47
  11.9 353.3 %all-gather.14.cloned.1.call-start = ((), (), s32[]{:S(2)}) async-start(), calls=%async_computation.10 | async-start | bytes 11837440 | tf_op jit(solution)/shard_map/all_gather | solution.py:51
  16.1 525.8 %all-gather.16.cloned.1.call-start = ((), (), s32[]{:S(2)}) async-start(), calls=%async_computation.11 | async-start | bytes 12533760 | tf_op jit(solution)/shard_map/all_gather | solution.py:53
  41.9 102.8 %copy-start.49 = (f32[1088]{0:T(1024)}, f32[1088]{0:T(1024)S(1)}, u32[]{:S(2)}) copy-start(f32[1088]{0:T(1024)S(1)} %convert_element_type.192) | copy-start | bytes 13060
  41.9 102.8 %copy-start.28 = (f32[1088]{0:T(1024)}, f32[1088]{0:T(1024)S(1)}, u32[]{:S(2)}) copy-start(f32[1088]{0:T(1024)S(1)} %convert_element_type.190) | copy-start | bytes 13060
  42.4 102.3 %copy-start.30 = (f32[1024]{0:T(1024)}, f32[1024]{0:T(1024)S(1)}, u32[]{:S(2)}) copy-start(f32[1024]{0:T(1024)S(1)} %broadcast_multiply_fusion.1) | copy-start | bytes 12292
  161.3 9.9 collective-permute-start
  166.9 929.8 %reduce-scatter.33.cloned.1.call-start = ((), (), s32[]{:S(2)}) async-start(), calls=%async_computation.21 | async-start | bytes 8460288
  336.0 253.1 %copy-start.38 = (f32[1024]{0:T(1024)}, f32[1024]{0:T(1024)S(1)}, u32[]{:S(2)}) copy-start(f32[1024]{0:T(1024)S(1)} %broadcast_multiply_fusion) | copy-start | bytes 12292
  338.6 250.5 %copy-start.46 = (f32[1024]{0:T(1024)}, f32[1024]{0:T(1024)S(1)}, u32[]{:S(2)}) copy-start(f32[1024]{0:T(1024)S(1)} %fusion.80) | copy-start | bytes 12292
  338.6 203.2 %copy-start.43 = (f32[4352]{0:T(1024)S(1)}, f32[4352]{0:T(1024)}, u32[]{:S(2)}) copy-start(f32[4352]{0:T(1024)} %convert_element_type.213) | copy-start | bytes 52228
  955.8 9.9 collective-permute-start.1
  988.2 191.2 %reduce-scatter.21.cloned.1.call-start = ((), (), s32[]{:S(2)}) async-start(), calls=%async_computation.12 | async-start | bytes 11280384 | tf_op jit(solution)/shard_map/reduce_scatter | solution.py:299
  1007.3 256.9 %reduce-scatter.23.cloned.1.call-start = ((), (), s32[]{:S(2)}) async-start(), calls=%async_computation.13 | async-start | bytes 10653696 | tf_op jit(solution)/shard_map/reduce_scatter | solution.py:302
  1026.0 285.7 %reduce-scatter.35.cloned.1.call-start = ((), (), s32[]{:S(2)}) async-start(), calls=%async_computation.22 | async-start | bytes 2820096
  1032.9 328.5 %reduce-scatter.25.cloned.1.call-start = ((), (), s32[]{:S(2)}) async-start(), calls=%async_computation.17 | async-start | bytes 2785280
  1099.4 319.0 %reduce-scatter.29.cloned.1.call-start = ((), (), s32[]{:S(2)}) async-start(), calls=%async_computation.19 | async-start | bytes 3481600
  1182.4 320.0 %reduce-scatter.31.cloned.1.call-start = ((), (), s32[]{:S(2)}) async-start(), calls=%async_computation.20 | async-start | bytes 5570560
  1268.0 154.0 %copy-start.56 = (bf16[1088]{0:T(1024)(128)(2,1)S(1)}, bf16[1088]{0:T(1024)(128)(2,1)}, u32[]{:S(2)}) copy-start(bf16[1088]{0:T(1024)(128)(2,1)} %get-tuple-element.350) | copy-start | bytes 6532
  1268.0 301.6 %reduce-scatter.27.cloned.1.call-start = ((), (), s32[]{:S(2)}) async-start(), calls=%async_computation.18 | async-start | bytes 1392640
  1313.9 271.9 %all-gather.20.cloned.1.call-start = ((), (), s32[]{:S(2)}) async-start(), calls=%async_computation.15 | async-start | bytes 2506752 | tf_op jit(solution)/shard_map/all_gather | solution.py:322
  1363.6 234.4 %all-gather.22.cloned.1.call-start = ((), (), s32[]{:S(2)}) async-start(), calls=%async_computation.16 | async-start | bytes 3133440 | tf_op jit(solution)/shard_map/all_gather | solution.py:328
  1420.7 209.4 %all-gather.18.cloned.1.call-start = ((), (), s32[]{:S(2)}) async-start(), calls=%async_computation.14 | async-start | bytes 2820096 | tf_op jit(solution)/shard_map/all_gather | solution.py:331
  (82 other events, 991.1 us)
Sparse Core Ops, SparseCore 0:
  10.9 133.7 all-gather.9
  146.3 50.9 all-gather.11
  198.8 166.3 all-gather.13
  367.2 174.6 all-gather.15
  988.3 108.3 reduce-scatter.32
  1100.2 79.1 reduce-scatter.20
  1183.3 80.7 reduce-scatter.22
  1268.6 43.0 reduce-scatter.34
  1314.7 46.7 reduce-scatter.24
  1364.3 54.0 reduce-scatter.28
  1421.3 80.9 reduce-scatter.30
  1505.1 28.4 reduce-scatter.26
  1536.2 26.8 all-gather.19
  1565.0 32.9 all-gather.21
  1600.4 29.6 all-gather.17
where the time goes:
time: 1650 us; the launch traced here: 1640 us
  waiting for transfers between devices  736 us (45%)
  matrix products  524 us (32%)
  other arithmetic  178 us (11%)
  local copies, waits for them, and re-layouts  95.7 us (6%)
  blocking collectives  75.8 us (5%)
  between operations  17.8 us (1%)
    unnamed x21, waiting for transfers between devices  266 us
    all_gather x1, waiting for transfers between devices, gather_first(): lax.all_gather(lows[11], 'fsdp', axis=0, tiled=True)  156 us
    all_gather x1, waiting for transfers between devices, gather_first(): lax.all_gather(lows[2], 'fsdp', axis=0, tiled=True)  101 us
    dot_general x4, matrix products, block_scores(): jnp.einsum('qhe,khe->hqk', query_block, key_block, preferred_element_type...  86.9 us
    convert_element_type x2, other arithmetic, backward_block(): grad_scores = (probability * (grad_prob - inner)).astype(jnp.bfloat16)  84.4 us
    dot_general x2, matrix products, backward_block(): jnp.einsum('qhe,khe->hqk', grad_out_block, value_block, preferred_element...  83.1 us
    reduce_scatter x1, waiting for transfers between devices, on_device(): lax.psum_scatter(grad_wproj.astype(jnp.bfloat16), 'ctx', scatter_dimensio...  81.7 us
    reduce_scatter x1, waiting for transfers between devices, on_device(): lax.psum_scatter(grad_wfc.astype(jnp.bfloat16), 'ctx', scatter_dimension=...  80 us
  transfers between devices with their start and end apart: 17, of which 14 were waited for; matrix products, arithmetic and copies ran while one was open for 22% of the time, Pallas kernels for 0%

commit v1 on v0

v1 whole, which is shorter than its diff:
```python
import math

import jax
import jax.numpy as jnp
from jax import lax
from jax.experimental import pallas as pl
from jax.experimental.pallas import tpu as pltpu
from jax.sharding import PartitionSpec as P

HEAD = 64
WINDOW = 1024
TILE = 128
ROWS = 256
LOG2E = 1.4426950408889634
epsilon = 1e-05
masked_score = -1e30
VMEM_BYTES = 60 * 1024 * 1024

NT = (((1,), (1,)), ((), ()))
TN = (((0,), (0,)), ((), ()))


def dot_f32(left, right, dims=(((1,), (0,)), ((), ()))):
    return lax.dot_general(left, right, dims, preferred_element_type=jnp.float32)


def head_lanes(rows, which):
    lane = lax.broadcasted_iota(jnp.int32, (rows, TILE), 1)
    return lane < HEAD if which == 0 else lane >= HEAD


def attention_forward_kernel(
    last, tok, q_ref, kh_ref, ko_ref, vh_ref, vo_ref, qdoc_ref, kdoc_ref,
    low_ref, full_ref, stat_ref, kcat, vcat,
):
    pair = pl.program_id(0)
    scale2 = LOG2E / math.sqrt(HEAD)
    span = ROWS + WINDOW

    @pl.when(pair == 0)
    def _():
        kcat[:, TILE:] = kdoc_ref[...]
        stat_ref[...] = jnp.zeros_like(stat_ref)

    kcat[:WINDOW, :TILE] = kh_ref[...]
    kcat[WINDOW:, :TILE] = ko_ref[...]
    vcat[:WINDOW] = vh_ref[...]
    vcat[WINDOW:] = vo_ref[...]
    row = lax.broadcasted_iota(jnp.int32, (ROWS, ROWS), 0)
    col = lax.broadcasted_iota(jnp.int32, (ROWS, ROWS), 1)
    lane = lax.broadcasted_iota(jnp.int32, (ROWS, TILE), 1)

    def one(block, which):
        rows = pl.ds(block * ROWS, ROWS)
        keys = pl.ds(block * ROWS, span)
        query = q_ref[rows, :]
        query = jnp.where(head_lanes(ROWS, which), query, jnp.zeros_like(query))
        query = jnp.concatenate([query, qdoc_ref[rows, :]], axis=1)
        scores = dot_f32(query, kcat[keys, :], NT)
        first = jnp.where(col >= row, scores[:, :ROWS], masked_score)
        final = jnp.where(col <= row, scores[:, WINDOW:], masked_score)
        scores = jnp.concatenate([first, scores[:, ROWS:WINDOW], final], axis=1)
        top = jnp.max(scores, axis=1, keepdims=True)
        expo = jnp.exp2((scores - top) * scale2)
        total = jnp.sum(expo, axis=1, keepdims=True)
        mixed = dot_f32(expo.astype(jnp.bfloat16), vcat[keys, :])
        stat = top * scale2 + jnp.log2(total)
        stat_ref[rows, :] = jnp.where(lane == 2 * pair + which, stat, stat_ref[rows, :])
        return mixed / total

    def block_out(heads):
        for block in range(tok // ROWS):
            rows = pl.ds(block * ROWS, ROWS)
            mixed = one(block, 0)
            other = one(block, 1) if heads == 2 else jnp.zeros_like(mixed)
            mixed = jnp.where(head_lanes(ROWS, 0), mixed, other)
            low_ref[rows, :] = mixed.astype(jnp.bfloat16)
            full_ref[rows, :] = mixed

    if last is None:
        block_out(2)
    else:
        pl.when(pair < last)(lambda: block_out(2))
        pl.when(pair == last)(lambda: block_out(1))


def attention_backward_kernel(
    last, tok, back, q_ref, kh_ref, ko_ref, vh_ref, vo_ref, do_ref, full_ref, lse_ref,
    qdoc_ref, kdoc_ref, dq_ref, dko_ref, dvo_ref,
    kcat, vcat, dk_acc, dv_acc, delta_ref,
):
    pair = pl.program_id(0)
    scale = 1.0 / math.sqrt(HEAD)
    scale2 = LOG2E * scale
    span = ROWS + WINDOW

    @pl.when(pair == 0)
    def _():
        kcat[:, TILE:] = kdoc_ref[...]

    kcat[:WINDOW, :TILE] = kh_ref[...]
    kcat[WINDOW:, :TILE] = ko_ref[...]
    vcat[:WINDOW] = vh_ref[...]
    vcat[WINDOW:] = vo_ref[...]
    dk_acc[...] = jnp.zeros_like(dk_acc)
    dv_acc[...] = jnp.zeros_like(dv_acc)
    key = lax.broadcasted_iota(jnp.int32, (ROWS, ROWS), 0)
    qry = lax.broadcasted_iota(jnp.int32, (ROWS, ROWS), 1)
    valid = head_lanes(tok, 0) | (pair < last if last is not None else True)
    product = jnp.where(valid, do_ref[...].astype(jnp.float32) * full_ref[...], 0.0)
    pick_row = lax.broadcasted_iota(jnp.int32, (8, TILE), 0)
    pick_lane = lax.broadcasted_iota(jnp.int32, (8, TILE), 1)
    pick = (pick_row == pick_lane // HEAD).astype(jnp.float32)
    delta_ref[...] = lax.dot_general(
        pick, product, NT, precision=lax.Precision.HIGHEST, preferred_element_type=jnp.float32
    )

    def one(block, which):
        rows = pl.ds(block * ROWS, ROWS)
        keys = pl.ds(block * ROWS, span)
        lanes = head_lanes(ROWS, which)
        query = q_ref[rows, :]
        query = jnp.where(lanes, query, jnp.zeros_like(query))
        upstream = do_ref[rows, :]
        upstream = jnp.where(lanes, upstream, jnp.zeros_like(upstream))
        query_doc = jnp.concatenate([query, qdoc_ref[rows, :]], axis=1)
        scores = dot_f32(kcat[keys, :], query_doc, NT)
        first = jnp.where(key >= qry, scores[:ROWS], masked_score)
        final = jnp.where(key <= qry, scores[WINDOW:], masked_score)
        scores = jnp.concatenate([first, scores[ROWS:WINDOW], final], axis=0)
        stat = lse_ref[0, which : which + 1, rows]
        delta = delta_ref[which : which + 1, rows]
        prob = jnp.exp2(scores * scale2 - stat)
        dprob = dot_f32(vcat[keys, :], upstream, NT)
        dscore = (prob * (dprob - delta)).astype(jnp.bfloat16)
        dv_acc[keys, :] += dot_f32(prob.astype(jnp.bfloat16), upstream)
        dk_acc[keys, :] += dot_f32(dscore, query)
        lanes_k = head_lanes(span, which)
        keys_one = kcat[keys, :TILE]
        keys_one = jnp.where(lanes_k, keys_one, jnp.zeros_like(keys_one))
        return dot_f32(dscore, keys_one, TN)

    def block_out(heads):
        for block in range(tok // ROWS):
            rows = pl.ds(block * ROWS, ROWS)
            dq = one(block, 0)
            if heads == 2:
                dq = dq + one(block, 1)
            dq_ref[rows, :] = (dq * scale).astype(jnp.bfloat16)

    if last is None:
        block_out(2)
    else:
        pl.when(pair < last)(lambda: block_out(2))
        pl.when(pair == last)(lambda: block_out(1))
    back.buf[pair, 0] = (dk_acc[:WINDOW] * scale).astype(jnp.bfloat16)
    back.buf[pair, 1] = dv_acc[:WINDOW].astype(jnp.bfloat16)
    back.send(pair)
    dko_ref[...] = (dk_acc[WINDOW:] * scale).astype(jnp.bfloat16)
    dvo_ref[...] = dv_acc[WINDOW:].astype(jnp.bfloat16)


def attention_forward(qkv, halo, qdoc, kdoc, features, engine, ident):
    tok = qkv.shape[0]
    pairs = -(-features // TILE)
    heads = features // HEAD
    last = pairs - 1 if heads % 2 else None
    blk = lambda off: pl.BlockSpec((tok, TILE), lambda p, off=off: (0, off + p))
    halo_blk = lambda off: pl.BlockSpec((WINDOW, TILE), lambda p, off=off: (0, off + p))
    fixed = lambda rows: pl.BlockSpec((rows, TILE), lambda p: (0, 0))
    return fused_call(
        lambda *refs: attention_forward_kernel(last, tok, *refs),
        pairs,
        (qkv, halo, qkv, halo, qkv, qdoc, kdoc),
        [
            blk(0), halo_blk(0), blk(pairs), halo_blk(pairs), blk(2 * pairs),
            fixed(tok), fixed(tok + WINDOW),
        ],
        [blk(0), blk(0), fixed(tok)],
        [
            jax.ShapeDtypeStruct((tok, features), jnp.bfloat16),
            jax.ShapeDtypeStruct((tok, pairs * TILE), jnp.float32),
            jax.ShapeDtypeStruct((tok, TILE), jnp.float32),
        ],
        [
            pltpu.VMEM((tok + WINDOW, 2 * TILE), jnp.bfloat16),
            pltpu.VMEM((tok + WINDOW, TILE), jnp.bfloat16),
        ],
        [engine],
        *gather_plan(engine, pairs),
        ident,
        cost=pl.CostEstimate(
            flops=4 * heads * tok * (ROWS + WINDOW) * HEAD * 4,
            bytes_accessed=tok * features * 20,
            transcendentals=heads * tok * (ROWS + WINDOW),
        ),
    )


def attention_backward(
    qkv, halo, upstream, full, lse, qdoc, kdoc, features, reduce, share, ident
):
    tok = qkv.shape[0]
    pairs = -(-features // TILE)
    heads = features // HEAD
    last = pairs - 1 if heads % 2 else None
    blk = lambda off: pl.BlockSpec((tok, TILE), lambda p, off=off: (0, off + p))
    halo_blk = lambda off: pl.BlockSpec((WINDOW, TILE), lambda p, off=off: (0, off + p))
    fixed = lambda rows: pl.BlockSpec((rows, TILE), lambda p: (0, 0))
    wide = pairs * TILE
    back = HaloBack(pairs, wide)
    schedule, end, done = reduce_plan(reduce, pairs, pairs - 3)
    those = range(len(share.jobs))
    schedule[3] += [call(lambda j: share.fetch(j).start(), j) for j in those]
    schedule[4] += [share.both(share.start, j) for j in those]
    schedule[7] += [share.both(share.across, j) for j in those]
    end += done + [share.both(share.finish, j) for j in those] + [back.finish]
    return fused_call(
        lambda *refs: attention_backward_kernel(last, tok, back, *refs),
        pairs,
        (qkv, halo, qkv, halo, qkv, upstream, full, lse, qdoc, kdoc),
        [
            blk(0), halo_blk(0), blk(pairs), halo_blk(pairs), blk(2 * pairs),
            blk(0), blk(0), pl.BlockSpec((1, 2, tok), lambda p: (p, 0, 0)),
            fixed(tok), fixed(tok + WINDOW),
        ],
        [blk(0), blk(0), blk(0)],
        [
            jax.ShapeDtypeStruct((tok, wide), jnp.bfloat16),
            jax.ShapeDtypeStruct((tok, wide), jnp.bfloat16),
            jax.ShapeDtypeStruct((tok, wide), jnp.bfloat16),
        ],
        [
            pltpu.VMEM((tok + WINDOW, 2 * TILE), jnp.bfloat16),
            pltpu.VMEM((tok + WINDOW, TILE), jnp.bfloat16),
            pltpu.VMEM((tok + WINDOW, TILE), jnp.float32),
            pltpu.VMEM((tok + WINDOW, TILE), jnp.float32),
            pltpu.VMEM((8, tok), jnp.float32),
        ],
        [reduce, share, back],
        schedule,
        end,
        ident,
        chain=True,
        cost=pl.CostEstimate(
            flops=10 * heads * tok * (ROWS + WINDOW) * HEAD * 4,
            bytes_accessed=tok * features * 40,
            transcendentals=heads * tok * (ROWS + WINDOW),
        ),
    )


GELU_A = math.sqrt(2.0 / math.pi)
GELU_B = 0.044715


def mlp_kernel(
    steps, opening, norm_ref, normt_ref, cot_ref, cott_ref, base_ref, dbase_ref, pbias_ref, fc_ref, fcb_ref, proj_ref,
    out_ref, dnorm_ref, gproj_ref, gfc_ref, gfcb_ref, final_acc, act_s, dpre_s,
):
    step = pl.program_id(0)
    tok = norm_ref.shape[0]

    @pl.when(step == 0)
    def _():
        final_acc[...] = base_ref[...]
        dnorm_ref[...] = jnp.zeros_like(dnorm_ref) if opening else dbase_ref[...]

    bias_sum = jnp.zeros(gfcb_ref.shape, jnp.float32)
    for part in range(tok // ROWS):
        rows = pl.ds(part * ROWS, ROWS)
        pre = dot_f32(norm_ref[rows, :], fc_ref[...]) + fcb_ref[...]
        dact = dot_f32(cot_ref[rows, :], proj_ref[...], NT)
        square = pre * pre
        bent = jnp.tanh(GELU_A * pre * (1.0 + GELU_B * square))
        half = 0.5 * (1.0 + bent)
        act = (pre * half).astype(jnp.bfloat16)
        slope = half + 0.5 * pre * (1.0 - bent * bent) * (
            GELU_A * (1.0 + 3.0 * GELU_B * square)
        )
        dpre = (dact * slope).astype(jnp.bfloat16)
        act_s[rows, :] = act
        dpre_s[rows, :] = dpre
        bias_sum = bias_sum + jnp.sum(dpre.astype(jnp.float32), axis=0, keepdims=True)
        final_acc[rows, :] += dot_f32(act, proj_ref[...])
        dnorm_ref[rows, :] += dot_f32(dpre, fc_ref[...], NT)
    gfcb_ref[...] = bias_sum
    gproj_ref[...] = dot_f32(cott_ref[...], act_s[...]).T.astype(jnp.bfloat16)
    gfc_ref[...] = dot_f32(normt_ref[...], dpre_s[...]).astype(jnp.bfloat16)

    if not opening:

        @pl.when(step == steps - 1)
        def _():
            for at in range(0, tok, ROWS):
                done = final_acc[at : at + ROWS, :] + pbias_ref[...]
                out_ref[:, at : at + ROWS] = done.T.astype(jnp.bfloat16)


def mlp_part(norm, norm_t, cot, cot_t, base, dbase, pbias, fc_w, fcb, proj_w, engine, schedule, end, ident):
    tok, features = norm.shape
    hidden = fc_w.shape[1]
    width = 256
    steps = hidden // width
    opening = dbase is None
    whole = lambda shape: pl.BlockSpec(shape, lambda j: (0, 0), pipeline_mode=pl.Buffered(1))
    cols = lambda rows: pl.BlockSpec((rows, width), lambda j: (0, j))
    rows = pl.BlockSpec((width, features), lambda j: (j, 0))

    def kern(*refs):
        refs = list(refs)
        if opening:
            refs.insert(5, None)
            refs.insert(6, None)
            refs.insert(15, refs[10])
        mlp_kernel(steps, opening, *refs)

    extra = [] if opening else [pltpu.VMEM((tok, features), jnp.float32)]
    return fused_call(
        kern,
        steps,
        (norm, norm_t, cot, cot_t, base) + (() if opening else (dbase, pbias)) + (fc_w, fcb, proj_w),
        [whole((tok, features)), whole((features, tok))] * 2
        + [whole((tok, features))] * (1 if opening else 2)
        + ([] if opening else [whole((1, features))])
        + [cols(features), cols(1), rows],
        [
            whole((tok, features) if opening else (features, tok)), whole((tok, features)), rows,
            cols(features), cols(1),
        ],
        [
            jax.ShapeDtypeStruct((tok, features), jnp.float32)
            if opening else jax.ShapeDtypeStruct((features, tok), jnp.bfloat16),
            jax.ShapeDtypeStruct((tok, features), jnp.float32),
            jax.ShapeDtypeStruct((hidden, features), jnp.bfloat16),
            jax.ShapeDtypeStruct((features, hidden), jnp.bfloat16),
            jax.ShapeDtypeStruct((1, hidden), jnp.float32),
        ],
        extra
        + [pltpu.VMEM((tok, width), jnp.bfloat16), pltpu.VMEM((tok, width), jnp.bfloat16)],
        [engine],
        schedule,
        end,
        ident,
        cost=pl.CostEstimate(
            flops=12 * tok * features * hidden,
            bytes_accessed=features * hidden * 8 + tok * features * 20,
            transcendentals=tok * hidden,
        ),
    )


def last_kernel(
    reduce, early, late, small, dims, normt_ref, xt_ref, gain_ref, dq_hbm, dk_hbm, dv_hbm, back_hbm, w_hbm,
    gresid_hbm, gout_hbm, fin_a, fin_b, small_hbm, out_hbm, rqkv_hbm, rout_hbm, ra_hbm, rb_hbm,
    small_out,
    g, back, w, resid, full, sums, column, sem_in, sem_out, *refs,
):
    features, tok, shards, wide = dims
    low = jnp.bfloat16
    own = []
    for engine in (reduce, early, late, small):
        own.append(refs[: len(engine.scratch)])
        refs = refs[len(engine.scratch) :]
    reduce.bind([full, gout_hbm], [], own[0])
    early.bind([fin_a, fin_b], [ra_hbm, rb_hbm], own[1])
    late.bind([], [rqkv_hbm, rout_hbm], own[2])
    small.bind([small_hbm], [small_out], own[3])
    ctx, last = lax.axis_index("ctx"), lax.axis_size("ctx") - 1
    loads = [
        pltpu.make_async_copy(src, dst, sem_in.at[n])
        for n, (src, dst) in enumerate((
            (dq_hbm, g.at[:, pl.ds(0, wide)]), (dk_hbm, g.at[:, pl.ds(wide, wide)]),
            (dv_hbm, g.at[:, pl.ds(2 * wide, wide)]), (back_hbm, back), (w_hbm, w),
            (gresid_hbm, resid),
        ))
    ]
    for item in loads:
        item.start()
    for j in (0, 1):
        early.fetch(j).start()
    small.load().start()
    sums[...] = jnp.zeros_like(sums)
    if g.shape[1] > 3 * wide:
        g[:, 3 * wide :] = jnp.zeros_like(g[:, 3 * wide :])
    greet()
    do = lambda action, *given: reduce.both(action, *given)()
    share = lambda engine, action, *given: engine.both(action, *given)()
    for s in range(shards):
        do(reduce.a_start, 1, s)
    for j in (0, 1):
        share(early, early.start, j)
    for item in loads[:4]:
        item.wait()

    @pl.when(ctx < last)
    def _():
        for at in range(0, tok, ROWS):
            some = slice(at, at + ROWS)
            for n in range(back.shape[0]):
                lanes = slice(wide + n * TILE, wide + (n + 1) * TILE)
                total = g[some, lanes].astype(jnp.float32) + back[n, some].astype(jnp.float32)
                g[some, lanes] = total.astype(low)

    def multiply(s):
        full[s] = dot_f32(normt_ref[reduce.owner(s)], g[...]).astype(low)
        do(reduce.a_start, 0, s)

    def columns():
        total = jnp.zeros((1, g.shape[1]), jnp.float32)
        for at in range(0, tok, ROWS):
            part = g[at : at + ROWS].astype(jnp.float32)
            total = total + jnp.sum(part, axis=0, keepdims=True)
        column[0:1] = total[:, :features]
        column[1:2] = total[:, 2 * wide : 2 * wide + features]

    def back_block(block):
        some = pl.ds(block * ROWS, ROWS)
        up = dot_f32(w[...], g[some, :], NT)
        x = xt_ref[:, some].astype(jnp.float32)
        centred = x - jnp.mean(x, axis=0, keepdims=True)
        inverse = lax.rsqrt(jnp.mean(centred * centred, axis=0, keepdims=True) + epsilon)
        hat = centred * inverse
        sums[:, 0:1] += jnp.sum(up * hat, axis=1, keepdims=True)
        sums[:, 1:2] += jnp.sum(up, axis=1, keepdims=True)
        up = up * gain_ref[...]
        lean = jnp.mean(up, axis=0, keepdims=True)
        tilt = jnp.mean(up * hat, axis=0, keepdims=True)
        resid[:, some] = resid[:, some] + inverse * (up - lean - hat * tilt)
        item = pltpu.make_async_copy(
            resid.at[:, some], out_hbm.at[:, some], sem_out.at[block]
        )
        item.start()
        return item

    multiply(0)
    for s in range(shards):
        do(reduce.b_start, 1, s)
    multiply(1)
    do(reduce.b_start, 0, 0)
    multiply(2)
    do(reduce.b_start, 0, 1)
    do(reduce.b_next, 1, 0)
    do(reduce.b_next, 1, 1)
    for s in range(3, shards):
        multiply(s)
    do(reduce.b_start, 0, 2)
    do(reduce.b_next, 0, 0)
    for s in range(2, shards):
        do(reduce.b_next, 1, s)
    for item in loads[4:]:
        item.wait()
    columns()
    for j in (0, 1):
        share(early, early.across, j)
    for s in range(3, shards):
        do(reduce.b_start, 0, s)
    saves = [back_block(0)]
    do(reduce.b_next, 0, 1)
    for s in range(shards):
        do(reduce.c_start, 1, s)
    saves.append(back_block(1))
    for s in range(2, shards):
        do(reduce.b_next, 0, s)
    do(reduce.c_start, 0, 0)
    saves.append(back_block(2))
    do(reduce.c_start, 0, 1)
    do(reduce.total, 1)
    share(late, late.start, 1)
    for block in range(3, tok // ROWS):
        saves.append(back_block(block))
    small.load().wait()
    small.own[0, 0:2] = sums[...].T[0:2]
    small.own[0, 2:4] = column[0:2]
    small.send(0)
    for s in range(2, shards):
        do(reduce.c_start, 0, s)
    small.add(0)
    small.send(1)
    do(reduce.total, 0)
    share(late, late.start, 0)
    small.add(1)
    small.send(2)
    share(late, late.across, 1)
    share(late, late.across, 0)
    small.add(2)
    small.finish()
    for j in (0, 1):
        share(early, early.finish, j)
        share(late, late.finish, j)
        do(reduce.finish, j)
    for item in saves:
        item.wait()


def last_call(
    jobs, early, normt, x_t, gain, dq, dk, dv, back, weights, gresid_t, gout, small, ident
):
    features, tok = x_t.shape
    shards = sizes()[1]
    wide, qkv_wide = dq.shape[1], weights.shape[1]
    low, struct = jnp.bfloat16, jax.ShapeDtypeStruct
    rows = features // shards
    reduce = ReduceHere(jobs, [struct((shards, rows, qkv_wide), low), gout], keep=False)
    late, tiny = Share(jobs, [], reduce), Small(small)
    vm = pl.BlockSpec(memory_space=pltpu.VMEM)
    dma = pltpu.SemaphoreType.DMA
    return pl.pallas_call(
        lambda *refs: last_kernel(
            reduce, early, late, tiny, (features, tok, shards, wide), *refs
        ),
        in_specs=[vm] * 3 + [any_spec()] * 10,
        out_specs=[any_spec()] * 6,
        out_shape=[struct((features, tok), jnp.float32)] + late.outs + early.outs + tiny.outs,
        scratch_shapes=[
            pltpu.VMEM((tok, qkv_wide), low), pltpu.VMEM(back.shape, low),
            pltpu.VMEM((features, qkv_wide), low), pltpu.VMEM((features, tok), jnp.float32),
            pltpu.VMEM((shards, rows, qkv_wide), low), pltpu.VMEM((features, TILE), jnp.float32),
            pltpu.VMEM((8, features), jnp.float32), dma((6,)), dma((tok // ROWS,)),
        ] + reduce.scratch + early.scratch + late.scratch + tiny.scratch,
        compiler_params=pltpu.CompilerParams(
            vmem_limit_bytes=VMEM_BYTES, collective_id=ident, has_side_effects=True
        ),
    )(
        normt.reshape(shards, rows, tok), x_t, gain, dq, dk, dv, back, weights, gresid_t, gout,
        *early.arrays, small,
    )


def at_step(schedule, end, steps, when, action):
    if when < steps:
        schedule.setdefault(when, []).append(action)
    else:
        end.append(action)


def gather_plan(engine, steps, deep=3):
    schedule, end = {0: [engine.open]}, []
    units = engine.units
    for unit in units[:deep]:
        schedule[0].append(engine.both(engine.start, *unit))
    count = len(units)
    late = []
    at_step(schedule, end, steps, 1, engine.keep)
    for n, unit in enumerate(units):
        when = 2 + n * (steps - 4) // count
        at_step(schedule, end, steps, when, engine.both(engine.spread, *unit))
        if n + deep < count:
            at_step(schedule, end, steps, when, engine.both(engine.start, *units[n + deep]))
        late.append((when + 1, engine.both(engine.relay, *unit)))
    for when, action in late:
        at_step(schedule, end, steps, when, action)
    for (when, _), unit in zip(late, units):
        at_step(schedule, end, steps, when + 1, engine.both(engine.across, *unit))
    end += [engine.both(engine.arrived, j) for j in range(len(engine.jobs))]
    end.append(engine.both(engine.close))
    return schedule, end


def reduce_plan(engine, steps, span):
    schedule, end = {}, []
    units = engine.units
    late, later = [], []
    for n, unit in enumerate(units):
        when = n * span // len(units)
        at_step(schedule, end, steps, when, engine.both(engine.a_start, *unit))
        late.append((when + 1, engine.both(engine.b_start, *unit)))
    for when, action in late:
        at_step(schedule, end, steps, when, action)
    for n, unit in enumerate(units):
        at_step(schedule, end, steps, n * span // len(units) + 2, engine.both(engine.b_next, *unit))
    for n, unit in enumerate(units):
        at_step(schedule, end, steps, n * span // len(units) + 3, engine.both(engine.c_start, *unit))
    jobs = range(len(engine.jobs))
    end += [engine.both(engine.total, j) for j in jobs]
    return schedule, end, [engine.both(engine.finish, j) for j in jobs]


def joined(ref, cols):
    shards, rows, _ = ref.shape
    value = ref[:, :, cols]
    if rows % 16:
        value = value.astype(jnp.float32)
    return value.reshape(shards * rows, value.shape[2]).astype(jnp.bfloat16)


def first_kernel(
    engine, dims, xt_ref, ct_ref, wqkv_ref, vec_ref, fc_hbm, proj_hbm, out_hbm,
    qkv_hbm, halo_hbm, normt_hbm, cot_hbm, vfull_ref, wfull_hbm, fca_hbm, fcb_hbm, pa_hbm, pb_hbm,
    outl_hbm, qkv_ref, halo_ref, normt_ref, cot_ref,
    wsrc, vsrc, xh, norm, normh, bias, fc32, proj32, out32, fca_s, fcb_s, pa_s, pb_s, outl_s,
    sem_in, sem_out, sem_x, sem_done, *sems,
):
    features, tok, shards, first, wide, chunk = dims
    low = jnp.bfloat16
    rows = wqkv_ref.shape[0]
    own = proj_hbm.shape[0]
    second = own - first
    parts = (wsrc.shape[1] + chunk - 1) // chunk
    wsrcs, ws, sems = sems[:parts], sems[parts : 2 * parts], sems[2 * parts :]
    engine.bind([vsrc] + list(wsrcs), [vfull_ref] + list(ws), sems)
    ctx, row, last = lax.axis_index("ctx"), lax.axis_index("fsdp"), lax.axis_size("ctx") - 1

    def load(n, src, dst):
        return pltpu.make_async_copy(src, dst, sem_in.at[n])

    cut = fc32.shape[0]
    deep = proj32.shape[0]
    loads = [
        load(0, fc_hbm.at[pl.ds(0, cut)], fc32), load(1, proj_hbm.at[pl.ds(0, deep)], proj32),
        load(2, out_hbm, out32),
    ]
    for item in loads:
        item.start()
    wsrc[...] = jnp.zeros_like(wsrc)
    for n in range(3):
        wsrc[:, n * wide : n * wide + features] = wqkv_ref[
            :, n * features : (n + 1) * features
        ].astype(low)
    vsrc[...] = vec_ref[...].astype(low)
    for n in range(parts):
        wsrcs[n][...] = wsrc[:, n * chunk : min((n + 1) * chunk, wsrc.shape[1])]
    greet(True)
    halo_copy = remote(
        xt_ref, xh, sem_x.at[0], sem_x.at[1], (jnp.minimum(ctx + 1, last), row)
    )
    units = engine.units
    engine.open()
    for unit in units[: shards - 1]:
        engine.both(engine.start, *unit)()
    done = []

    def ready(n, src, dst):
        item = pltpu.make_async_copy(src, dst, sem_done.at[n])
        item.start()
        done.append(item)

    @pl.when(ctx == 0)
    def _():
        xh[...] = jnp.zeros_like(xh)

    saves = [
        pltpu.make_async_copy(src, dst, sem_out.at[n])
        for n, (src, dst) in enumerate(
            ((fca_s, fca_hbm), (fcb_s, fcb_hbm), (pa_s, pa_hbm), (pb_s, pb_hbm),
             (outl_s, outl_hbm))
        )
    ]

    def cast_fc(at):
        load(0, fc_hbm.at[pl.ds(at, cut)], fc32).wait()
        for n in range(shards):
            fca_s[at : at + cut, n * first : (n + 1) * first] = fc32[
                :, n * own : n * own + first
            ].astype(low)
            fcb_s[at : at + cut, n * second : (n + 1) * second] = fc32[
                :, n * own + first : (n + 1) * own
            ].astype(low)
        if at + cut < rows:
            load(0, fc_hbm.at[pl.ds(at + cut, cut)], fc32).start()

    def cast_proj(at):
        load(1, proj_hbm.at[pl.ds(at, deep)], proj32).wait()
        stop = min(max(first - at, 0), deep)
        if stop:
            pa_s[at : at + stop] = proj32[:stop].astype(low)
        if stop < deep:
            pb_s[at + stop - first : at + deep - first] = proj32[stop:].astype(low)
        if at + deep < own:
            load(1, proj_hbm.at[pl.ds(at + deep, deep)], proj32).start()

    def cast_out():
        load(2, out_hbm, out32).wait()
        outl_s[...] = jnp.zeros_like(outl_s)
        outl_s[:, :features] = out32[...].astype(low)
        for item in saves:
            item.start()

    def turn_cot():
        for at in range(0, tok, ROWS):
            cot_ref[at : at + ROWS, :] = ct_ref[:, at : at + ROWS].T
        ready(3, cot_ref, cot_hbm)

    def vectors():
        engine.both(engine.arrived, 0)()
        engine.local(0).wait()
        columns = vfull_ref[...].astype(jnp.float32).reshape(features, vfull_ref.shape[2])
        columns = columns[:, :TILE]
        lines = columns.T
        bias[...] = jnp.zeros_like(bias)
        bias[0:1, :features] = lines[2:3]
        bias[0:1, 2 * wide : 2 * wide + features] = lines[3:4]
        return columns

    def normalise(src, columns, dst, dst_t):
        gain, shift = columns[:, 0:1], columns[:, 1:2]
        for at in range(0, tok, ROWS):
            x = src[:, at : at + ROWS].astype(jnp.float32)
            centred = x - jnp.mean(x, axis=0, keepdims=True)
            spread = jnp.mean(centred * centred, axis=0, keepdims=True)
            y = centred * lax.rsqrt(spread + epsilon) * gain + shift
            if dst_t is not None:
                dst_t[:, at : at + ROWS] = y.astype(low)
            dst[at : at + ROWS, :] = y.T.astype(low)

    def multiply(n):
        engine.both(engine.arrived, 1 + n)()
        engine.local(1 + n).wait()
        lo, hi = n * chunk, min((n + 1) * chunk, wsrc.shape[1])
        weights = joined(ws[n], slice(0, hi - lo))
        item = pltpu.make_async_copy(
            ws[n], wfull_hbm.at[:, :, pl.ds(lo, hi - lo)], sem_done.at[12 + n]
        )
        item.start()
        done.append(item)
        for at in range(0, tok, ROWS):
            part = dot_f32(norm[at : at + ROWS, :], weights) + bias[0:1, lo:hi]
            qkv_ref[at : at + ROWS, lo:hi] = part.astype(low)
        ready(4 + 2 * n, qkv_ref.at[:, pl.ds(lo, hi - lo)], qkv_hbm.at[:, pl.ds(lo, hi - lo)])
        lo_h, hi_h = max(lo, wide), min(hi, 3 * wide)
        if lo_h >= hi_h:
            return
        weights = weights[:, lo_h - lo : hi_h - lo]
        for at in range(0, tok, ROWS):
            part = dot_f32(normh[at : at + ROWS, :], weights) + bias[0:1, lo_h:hi_h]
            halo_ref[at : at + ROWS, lo_h - wide : hi_h - wide] = part.astype(low)
        span = pl.ds(lo_h - wide, hi_h - lo_h)
        ready(5 + 2 * n, halo_ref.at[:, span], halo_hbm.at[:, span])

    per = shards - 1
    groups = [units[n : n + per] for n in range(0, len(units), per)]
    chunks = groups[1:]

    def each(action, group):
        for unit in group:
            engine.both(action, *unit)()

    for group in chunks[:2]:
        each(engine.start, group)
    pl.when(ctx < last)(lambda: halo_copy.start())
    for at in range(0, rows, cut):
        cast_fc(at)
    each(engine.spread, groups[0])
    each(engine.spread, chunks[0])
    for at in range(0, own, deep):
        cast_proj(at)
    cast_out()
    each(engine.relay, groups[0])
    each(engine.relay, chunks[0])
    each(engine.spread, chunks[1])
    each(engine.start, chunks[2])
    turn_cot()
    each(engine.across, groups[0])
    each(engine.across, chunks[0])
    each(engine.relay, chunks[1])
    each(engine.start, chunks[3])
    columns = vectors()
    normalise(xt_ref, columns, norm, normt_ref)
    ready(2, normt_ref, normt_hbm)
    each(engine.spread, chunks[2])
    each(engine.across, chunks[1])
    multiply(0)
    each(engine.spread, chunks[3])
    each(engine.relay, chunks[2])

    @pl.when(ctx > 0)
    def _():
        halo_copy.wait_recv()

    normalise(xh, columns, normh, None)
    each(engine.relay, chunks[3])
    each(engine.across, chunks[2])
    multiply(1)
    each(engine.across, chunks[3])
    multiply(2)
    multiply(3)
    engine.both(engine.close)()
    pl.when(ctx < last)(lambda: halo_copy.wait_send())
    for item in saves + done:
        item.wait()


def first_call(xt, ct, w_qkv, vec, w_fc, w_proj, w_out, first, wide, qkv_wide, out_wide, ident):
    features, tok = xt.shape
    planes, shards = sizes()
    rows, own = w_qkv.shape[0], w_proj.shape[0]
    low = jnp.bfloat16
    chunk = CORES * 4 * TILE
    columns = vec.shape[1]
    struct = jax.ShapeDtypeStruct
    wides = [columns] + [min(chunk, qkv_wide - at) for at in range(0, qkv_wide, chunk)]
    jobs = [best_job(rows, n) for n in wides]
    engine = GatherHere(jobs, [struct((rows, n), low) for n in wides], list(range(len(jobs))))
    dims = features, tok, shards, first, wide, chunk
    vm = pl.BlockSpec(memory_space=pltpu.VMEM)
    second = own - first
    cut = rows // 2 if rows // 2 % 8 == 0 else rows
    dma = pltpu.SemaphoreType.DMA
    return pl.pallas_call(
        lambda *refs: first_kernel(engine, dims, *refs),
        in_specs=[vm] * 4 + [any_spec()] * 3,
        out_specs=[any_spec()] * 4 + [vm] + [any_spec()] * 6,
        out_shape=[
            struct((tok, qkv_wide), low), struct((tok, 2 * wide), low), struct((features, tok), low),
            struct((tok, features), low), struct((shards, rows, columns), low),
            struct((shards, rows, qkv_wide), low), struct((rows, shards * first), low),
            struct((rows, shards * second), low), struct((first, features), low),
            struct((second, features), low), struct((rows, out_wide), low),
        ],
        scratch_shapes=[
            pltpu.VMEM((tok, qkv_wide), low), pltpu.VMEM((tok, 2 * wide), low),
            pltpu.VMEM((features, tok), low), pltpu.VMEM((tok, features), low),
            pltpu.VMEM((rows, qkv_wide), low),
            pltpu.VMEM((rows, columns), low), pltpu.VMEM((features, tok), low),
            pltpu.VMEM((tok, features), low), pltpu.VMEM((tok, features), low),
            pltpu.VMEM((8, qkv_wide), jnp.float32), pltpu.VMEM((cut, w_fc.shape[1]), jnp.float32),
            pltpu.VMEM((own // 2, features), jnp.float32),
            pltpu.VMEM((rows, features), jnp.float32),
            pltpu.VMEM((rows, shards * first), low), pltpu.VMEM((rows, shards * second), low),
            pltpu.VMEM((first, features), low), pltpu.VMEM((second, features), low),
            pltpu.VMEM((rows, out_wide), low), dma((3,)), dma((6,)), dma((2,)),
            dma((16,)),
        ] + [pltpu.VMEM((rows, n), low) for n in wides[1:]]
        + [pltpu.VMEM((shards, rows, n), low) for n in wides[1:]] + engine.scratch,
        compiler_params=pltpu.CompilerParams(
            vmem_limit_bytes=VMEM_BYTES, collective_id=ident, has_side_effects=True
        ),
    )(xt, ct, w_qkv, vec, w_fc, w_proj, w_out)


def final_kernel(
    features, shards, qkv_ref, out_ref, fca_ref, fcb_ref, pa_ref, pb_ref,
    gqkv_ref, gout_ref, gfc_ref, gproj_ref,
):
    step = pl.program_id(0)
    wide = -(-features // TILE) * TILE
    for n in range(3):
        gqkv_ref[:, n * features : (n + 1) * features] = qkv_ref[
            :, n * wide : n * wide + features
        ].astype(jnp.float32)
    gout_ref[...] = out_ref[:, :features].astype(jnp.float32)
    own, first = gfc_ref.shape[1] // shards, fca_ref.shape[1] // shards
    second = own - first
    for n in range(shards):
        gfc_ref[:, n * own : n * own + first] = fca_ref[
            :, n * first : (n + 1) * first
        ].astype(jnp.float32)
        gfc_ref[:, n * own + first : (n + 1) * own] = fcb_ref[
            :, n * second : (n + 1) * second
        ].astype(jnp.float32)
    rows = gproj_ref.shape[0]

    def proj(at):
        stop = min(max(first - at * rows, 0), rows)
        if stop:
            gproj_ref[:stop] = pa_ref[at * rows : at * rows + stop].astype(jnp.float32)
        if stop < rows:
            low = at * rows + stop - first
            gproj_ref[stop:] = pb_ref[low : low + rows - stop].astype(jnp.float32)

    for at in range(own // rows):
        pl.when(step == at)(call(proj, at))


def finals(features, shards, r_qkv, r_out, r_fca, r_fcb, r_proja, r_projb):
    rows, own = r_qkv.shape[0], r_proja.shape[0] + r_projb.shape[0]
    steps = 2 if rows // 2 % 8 == 0 else 1
    blk = lambda a: pl.BlockSpec((rows // steps, a.shape[1]), lambda i: (i, 0))
    whole = lambda a: pl.BlockSpec(a.shape, lambda i: (0, 0), pipeline_mode=pl.Buffered(1))
    shapes = [(rows, 3 * features), (rows, features), (rows, own * shards), (own, features)]
    return pl.pallas_call(
        lambda *refs: final_kernel(features, shards, *refs),
        grid=(steps,),
        in_specs=[blk(a) for a in (r_qkv, r_out, r_fca, r_fcb)]
        + [whole(r_proja), whole(r_projb)],
        out_specs=[pl.BlockSpec((s[0] // steps, s[1]), lambda i: (i, 0)) for s in shapes],
        out_shape=[jax.ShapeDtypeStruct(s, jnp.float32) for s in shapes],
        compiler_params=pltpu.CompilerParams(vmem_limit_bytes=VMEM_BYTES),
    )(r_qkv, r_out, r_fca, r_fcb, r_proja, r_projb)


def out_norm_kernel(att_ref, w_ref, xt_ref, vec_ref, resid_ref, norm_ref, normt_ref):
    features = resid_ref.shape[1]
    mixed = dot_f32(att_ref[...], w_ref[...])[:, :features] + vec_ref[0:1]
    resid = xt_ref[...].astype(jnp.float32).T + mixed
    resid_ref[...] = resid
    centred = resid - jnp.mean(resid, axis=1, keepdims=True)
    spread = jnp.mean(centred * centred, axis=1, keepdims=True)
    normed = centred * lax.rsqrt(spread + epsilon) * vec_ref[1:2] + vec_ref[2:3]
    norm_ref[...] = normed.astype(jnp.bfloat16)
    normt_ref[...] = normed.T.astype(jnp.bfloat16)


def out_norm(attended, out_w, x_t, vec):
    tok, features = attended.shape
    blk = pl.BlockSpec((ROWS, features), lambda i: (i, 0))
    blk_t = pl.BlockSpec((features, ROWS), lambda i: (0, i))
    whole = lambda a: pl.BlockSpec(a.shape, lambda i: (0, 0), pipeline_mode=pl.Buffered(1))
    struct = jax.ShapeDtypeStruct
    return pl.pallas_call(
        out_norm_kernel,
        grid=(tok // ROWS,),
        in_specs=[blk, whole(out_w), blk_t, whole(vec)],
        out_specs=[blk, blk, blk_t],
        out_shape=[
            struct((tok, features), jnp.float32), struct((tok, features), jnp.bfloat16),
            struct((features, tok), jnp.bfloat16),
        ],
        compiler_params=pltpu.CompilerParams(vmem_limit_bytes=VMEM_BYTES),
    )(attended, out_w, x_t, vec)


def middle_kernel(
    steps, dnorm_ref, resid_ref, cot_ref, att_ref, w_ref, vec_ref,
    gresid_ref, datt_ref, gout_ref, sums_ref, branch_t,
):
    step = pl.program_id(0)
    features = resid_ref.shape[1]

    @pl.when(step == 0)
    def _():
        sums_ref[...] = jnp.zeros_like(sums_ref)

    up, resid = dnorm_ref[...], resid_ref[...]
    cot = cot_ref[...].astype(jnp.float32)
    centred = resid - jnp.mean(resid, axis=1, keepdims=True)
    inverse = lax.rsqrt(jnp.mean(centred * centred, axis=1, keepdims=True) + epsilon)
    hat = centred * inverse
    sums_ref[0:1] += jnp.sum(up * hat, axis=0, keepdims=True)
    sums_ref[1:2] += jnp.sum(up, axis=0, keepdims=True)
    sums_ref[3:4] += jnp.sum(cot, axis=0, keepdims=True)
    up = up * vec_ref[1:2]
    lean = jnp.mean(up, axis=1, keepdims=True)
    tilt = jnp.mean(up * hat, axis=1, keepdims=True)
    gresid = cot + inverse * (up - lean - hat * tilt)
    turned = gresid.T
    gresid_ref[...] = turned
    branch = gresid.astype(jnp.bfloat16)
    branch_t[:, pl.ds(pl.multiple_of(step * ROWS, ROWS), ROWS)] = turned.astype(jnp.bfloat16)
    sums_ref[2:3] += jnp.sum(branch.astype(jnp.float32), axis=0, keepdims=True)
    datt_ref[...] = dot_f32(branch, w_ref[:, :features], NT).astype(jnp.bfloat16)

    @pl.when(step == steps - 1)
    def _():
        gout_ref[:, features:] = jnp.zeros_like(gout_ref[:, features:])
        for at in range(0, features, ROWS):
            some = slice(at, min(at + ROWS, features))
            grad = dot_f32(branch_t[some, :], att_ref[...])
            gout_ref[:, some] = grad.T.astype(jnp.bfloat16)


def middle(dnorm, resid, cot, attended, out_w, vec):
    tok, features = resid.shape
    steps = tok // ROWS
    blk = pl.BlockSpec((ROWS, features), lambda i: (i, 0))
    blk_t = pl.BlockSpec((features, ROWS), lambda i: (0, i))
    whole = lambda shape: pl.BlockSpec(shape, lambda i: (0, 0), pipeline_mode=pl.Buffered(1))
    struct = jax.ShapeDtypeStruct
    return pl.pallas_call(
        lambda *refs: middle_kernel(steps, *refs),
        grid=(steps,),
        in_specs=[blk, blk, blk, whole(attended.shape), whole(out_w.shape), whole(vec.shape)],
        out_specs=[blk_t, blk, whole(out_w.shape), whole((8, features))],
        out_shape=[
            struct((features, tok), jnp.float32), struct((tok, features), jnp.bfloat16),
            struct(out_w.shape, jnp.bfloat16), struct((8, features), jnp.float32),
        ],
        scratch_shapes=[pltpu.VMEM((features, tok), jnp.bfloat16)],
        compiler_params=pltpu.CompilerParams(
            vmem_limit_bytes=VMEM_BYTES, fuse_transposed_lhs_in_matmul=True
        ),
    )(dnorm, resid, cot, attended, out_w, vec)


MESH = pl.DeviceIdType.MESH
CORES = 2


def place():
    ctx, row = lax.axis_index("ctx"), lax.axis_index("fsdp")
    planes, shards = lax.axis_size("ctx") // CORES, lax.axis_size("fsdp")
    return ctx // CORES, lax.rem(ctx, CORES), row, planes, shards


def plane_peer(plane, core, row, planes, by):
    return (lax.rem(plane + by, planes) * CORES + core, row)


def greet(chain=False):
    plane, core, row, planes, shards = place()
    ctx = plane * CORES + core
    barrier = pltpu.get_barrier_semaphore()
    if chain:
        last = planes * CORES - 1

        @pl.when(ctx > 0)
        def _():
            pl.semaphore_signal(barrier, inc=1, device_id=(ctx - 1, row), device_id_type=MESH)

        @pl.when(ctx < last)
        def _():
            pl.semaphore_signal(barrier, inc=1, device_id=(ctx + 1, row), device_id_type=MESH)

    peers = [(plane * CORES + 1 - core, row)]
    peers += [plane_peer(plane, core, row, planes, by) for by in range(1, planes)]
    peers += [(ctx, lax.rem(row + by, shards)) for by in range(1, shards)]
    for peer in peers:
        pl.semaphore_signal(barrier, inc=1, device_id=peer, device_id_type=MESH)
    if chain:
        near = jnp.where(ctx > 0, 1, 0) + jnp.where(ctx < last, 1, 0)
        pl.semaphore_wait(barrier, len(peers) + near)
    else:
        pl.semaphore_wait(barrier, len(peers))


class Job:
    def __init__(self, axis, rows, columns, first=0, share=0.5):
        self.axis, self.rows, self.columns, self.first = axis, rows, columns, first
        self.grain = 128 if axis else 16
        total = (columns if axis else rows) // self.grain
        assert total * self.grain == (columns if axis else rows)
        front = round(total * share)
        self.halves = front, total - front
        self.starts = 0, front
        self.half = front if front * CORES == total else None

    def span(self, start, size):
        start = start * self.grain
        if not isinstance(start, int):
            start = pl.multiple_of(start, self.grain)
        return pl.ds(start, size * self.grain)

    def cut(self, ref, start, size):
        span = self.span(start, size)
        return ref.at[:, span] if self.axis else ref.at[span, :]

    def index(self, start, size):
        span = self.span(start, size)
        return (slice(None), span) if self.axis else (span, slice(None))

    def shape(self, size):
        size = size * self.grain
        return (self.rows, size) if self.axis else (size, self.columns)

    def parts(self, planes, plane, core=0):
        base, extra = divmod(self.halves[core], planes)
        start = plane * base + jnp.minimum(plane, extra)
        found = []
        if base:
            found.append((start, base, None, 0))
        if extra:
            found.append((start + base, 1, plane < extra, base))
        return found

    def piece(self, planes):
        return -(-max(self.halves) // planes)


def flip(plane, bit):
    one = plane + 1 - 2 * lax.rem(plane, 2)
    if isinstance(bit, int):
        return one if bit == 1 else lax.rem(plane + 2, 4)
    return one * (2 - bit) + lax.rem(plane + 2, 4) * (bit - 1)


def guarded(cond, action):
    if cond is None:
        action()
    else:
        pl.when(cond)(action)


def remote(src, dst, send, recv, peer):
    return pltpu.make_async_remote_copy(
        src_ref=src, dst_ref=dst, send_sem=send, recv_sem=recv, device_id=peer,
        device_id_type=MESH,
    )


def best_job(rows, columns, share=0.5):
    return Job(0 if rows % 16 == 0 else 1, rows, columns, 0, share)


class Engine:
    def both(self, action, *given):
        def run():
            core = self.core

            def at(which):
                def branch():
                    self.core = which
                    action(*given)
                return branch

            pl.when(core == 0)(at(0))
            pl.when(core != 0)(at(1))
            self.core = core

        return run


class Gather(Engine):
    def __init__(self, jobs, arrays, owners=None):
        self.jobs, self.arrays = jobs, arrays
        self.owners = owners or list(range(len(jobs)))
        planes, shards = sizes()
        count = len(jobs)
        dma = pltpu.SemaphoreType.DMA
        self.outs = [jax.ShapeDtypeStruct((shards,) + a.shape, a.dtype) for a in arrays]
        self.scratch = [
            dma((count, shards, 2, 2)), dma((count, shards, max(planes, 5), 2, 2)),
            dma((count, shards, 2)), dma((len(arrays), 2)),
        ] + [pltpu.VMEM(a.shape, a.dtype) for a in arrays]
        self.units = [(j, by) for j in range(count) for by in range(1, shards)]

    def bind(self, srcs, dsts, sems):
        self.all_srcs, self.all_dsts = srcs, dsts
        self.srcs = [srcs[n] for n in self.owners]
        self.dsts = [dsts[n] for n in self.owners]
        self.sem_z, self.sem_p, self.sem_c, self.sem_l = sems[:4]
        self.staged = sems[4:]
        self.plane, self.core, self.row, self.planes, self.shards = place()

    def mine(self, j, plane=None):
        job = self.jobs[j]
        plane = self.plane if plane is None else plane
        for i, (start, size, cond, _) in enumerate(job.parts(self.planes, plane, self.core)):
            yield i, start + job.starts[self.core] + job.first, size, cond

    def fetch(self, n):
        return pltpu.make_async_copy(self.all_srcs[n], self.staged[n], self.sem_l.at[n, 0])

    def local(self, n):
        return pltpu.make_async_copy(
            self.staged[n], self.all_dsts[n].at[self.row], self.sem_l.at[n, 1]
        )

    def turn(self, by):
        return by + self.core * (self.shards - 2 * by)

    def origin(self, by):
        return lax.rem(self.row + self.shards - by, self.shards)

    def copy_z(self, j, by, i, start, size, incoming):
        job = self.jobs[j]
        sems = self.sem_z.at[j, by, i, 0], self.sem_z.at[j, by, i, 1]
        peer = (self.plane * CORES + self.core, lax.rem(self.row + by, self.shards))
        if incoming:
            ref = job.cut(self.dsts[j].at[self.origin(by)], start, size)
            return remote(ref, ref, *sems, peer)
        src = job.cut(self.srcs[j], start, size)
        return remote(src, job.cut(self.dsts[j].at[self.row], start, size), *sems, peer)

    def half(self, ref, job, part):
        if job.axis:
            cut = -(-job.rows // 32) * 16
            return ref.at[pl.ds(0, cut)] if part == 0 else ref.at[pl.ds(cut, job.rows - cut)]
        cut = -(-job.columns // 256) * 128
        if part == 0:
            return ref.at[:, pl.ds(0, cut)]
        return ref.at[:, pl.ds(cut, job.columns - cut)]

    def copy_p(self, j, by, q, i, start, size):
        job = self.jobs[j]
        sems = self.sem_p.at[j, by, q, i, 0], self.sem_p.at[j, by, q, i, 1]
        ref = job.cut(self.dsts[j].at[self.origin(by)], start, size)
        if self.planes != 4:
            peer = plane_peer(self.plane, self.core, self.row, self.planes, q)
            return remote(ref, ref, *sems, peer)
        if q > 2:
            ref, q = self.half(ref, job, q - 3), q - 2
        return remote(ref, ref, *sems, (flip(self.plane, q) * CORES + self.core, self.row))

    def copy_c(self, j, by, core):
        job = self.jobs[j]
        start = job.starts[core] + job.first
        ref = job.cut(self.dsts[j].at[self.origin(by)], start, job.halves[core])
        peer = (self.plane * CORES + 1 - self.core, self.row)
        return remote(ref, ref, self.sem_c.at[j, by, 0], self.sem_c.at[j, by, 1], peer)

    def open(self):
        for n in range(len(self.arrays)):
            self.fetch(n).start()

    def keep(self):
        for n in range(len(self.arrays)):
            self.fetch(n).wait()
            self.local(n).start()

    def start(self, j, by):
        by = self.turn(by)
        for i, start, size, cond in self.mine(j):
            guarded(cond, lambda: self.copy_z(j, by, i, start, size, False).start())

    def by_core(self, first, second):
        @pl.when(self.core == 0)
        def _():
            first()
            second()

        @pl.when(self.core != 0)
        def _():
            second()
            first()

    def spread(self, j, by):
        by = self.turn(by)
        for i, start, size, cond in self.mine(j):
            def forward():
                self.copy_z(j, by, i, start, size, True).wait_recv()
                if self.planes == 4:
                    self.by_core(
                        self.copy_p(j, by, 1, i, start, size).start,
                        lambda: self.copy_p(j, by, 2, i, start, size).start(),
                    )
                else:
                    for q in range(1, self.planes):
                        self.copy_p(j, by, q, i, start, size).start()
            guarded(cond, forward)

    def relay(self, j, by):
        if self.planes != 4:
            return
        by = self.turn(by)

        def one(bit):
            def run():
                for i, start, size, cond in self.mine(j, plane=flip(self.plane, bit)):
                    def pass_on():
                        self.copy_p(j, by, bit, i, start, size).wait_recv()
                        self.copy_p(j, by, 5 - bit, i, start, size).start()
                    guarded(cond, pass_on)
            return run

        self.by_core(one(2), one(1))

    def across(self, j, by):
        by = self.turn(by)
        if self.planes == 4:
            for i, start, size, cond in self.mine(j, plane=flip(flip(self.plane, 1), 2)):
                def both():
                    for q in (3, 4):
                        self.copy_p(j, by, q, i, start, size).wait_recv()
                guarded(cond, both)
        else:
            for q in range(1, self.planes):
                origin = lax.rem(self.plane + self.planes - q, self.planes)
                for i, start, size, cond in self.mine(j, plane=origin):
                    guarded(cond, lambda: self.copy_p(j, by, q, i, start, size).wait_recv())
        self.copy_c(j, by, self.core).start()

    def arrived(self, j):
        for by in range(1, self.shards):
            self.copy_c(j, by, 1 - self.core).wait_recv()

    def close(self):
        for j, by in self.units:
            self.copy_c(j, by, self.core).wait_send()
            for i, start, size, cond in self.mine(j):
                def sent():
                    self.copy_z(j, by, i, start, size, False).wait_send()
                    for q in (1, 2) if self.planes == 4 else range(1, self.planes):
                        self.copy_p(j, by, q, i, start, size).wait_send()
                guarded(cond, sent)
            if self.planes == 4:
                for bit in (1, 2):
                    for i, start, size, cond in self.mine(j, plane=flip(self.plane, bit)):
                        guarded(
                            cond,
                            lambda: self.copy_p(j, by, 5 - bit, i, start, size).wait_send(),
                        )
        self.settle()

    def settle(self):
        for n in range(len(self.arrays)):
            self.local(n).wait()


class GatherHere(Gather):
    def __init__(self, jobs, arrays, owners):
        super().__init__(jobs, arrays, owners)
        self.scratch = self.scratch[:4]

    def local(self, n):
        return pltpu.make_async_copy(
            self.all_srcs[n], self.all_dsts[n].at[self.row], self.sem_l.at[n, 1]
        )

    def open(self):
        for n in range(len(self.arrays)):
            self.local(n).start()

    def keep(self):
        pass

    def settle(self):
        pass


class Reduce(Engine):
    def __init__(self, jobs, arrays, keep=True, near=0):
        self.jobs, self.arrays, self.keep, self.near = jobs, arrays, keep, near
        planes, shards = sizes()
        count = len(jobs)
        dma = pltpu.SemaphoreType.DMA
        low = jnp.bfloat16
        refs = []
        for job in jobs:
            piece = job.piece(planes)
            refs += [
                pltpu.VMEM((shards,) + job.shape(max(job.halves)), low),
                pltpu.VMEM((shards,) + job.shape(max(job.halves)), low),
                pltpu.VMEM((shards, planes - 1) + job.shape(piece), low),
                pltpu.VMEM((shards,) + job.shape(piece), low),
                pltpu.VMEM((shards - 1,) + job.shape(piece), low),
            ]
        self.outs = [
            jax.ShapeDtypeStruct(job.shape(job.piece(planes)), low) for job in jobs if keep
        ]
        self.scratch = refs + [
            dma((count, shards, 3)), dma((count, shards, planes, 2, 2)),
            dma((count, shards, 2, 2)), dma((count,)),
        ]
        self.units = [(j, s) for s in range(shards) for j in range(count)]

    def bind(self, grads, outs, refs):
        count = len(self.jobs)
        self.grads, self.fins = grads, outs
        self.bufs = [refs[5 * j : 5 * j + 5] for j in range(count)]
        self.sem_a, self.sem_b, self.sem_c, self.sem_f = refs[5 * count :]
        self.plane, self.core, self.row, self.planes, self.shards = place()

    def owner(self, s):
        return lax.rem(self.row + 1 + s, self.shards)

    def sibling(self):
        return (self.plane * CORES + 1 - self.core, self.row)

    def locate(self, j, s):
        return self.grads[j].at[self.owner(s)]

    def copy_a(self, j, s, core):
        job = self.jobs[j]
        src = job.cut(self.locate(j, s), job.starts[core], job.halves[core])
        dst = job.cut(self.bufs[j][1].at[s], 0, job.halves[core])
        return remote(
            src, dst, self.sem_a.at[j, s, 0], self.sem_a.at[j, s, 1], self.sibling()
        )

    def load_a(self, j, s):
        job = self.jobs[j]
        src = job.cut(self.locate(j, s), job.starts[self.core], job.halves[self.core])
        dst = job.cut(self.bufs[j][0].at[s], 0, job.halves[self.core])
        return pltpu.make_async_copy(src, dst, self.sem_a.at[j, s, 2])

    def copy_b(self, j, s, slot, peer, i, start, size, at):
        job = self.jobs[j]
        src = job.cut(self.bufs[j][0].at[s], start, size)
        dst = job.cut(self.bufs[j][2].at[s, slot], at, size)
        sems = self.sem_b.at[j, s, slot, i, 0], self.sem_b.at[j, s, slot, i, 1]
        return remote(src, dst, *sems, (peer * CORES + self.core, self.row))

    def sends(self, j, s, second):
        if self.planes != 4:
            return [] if second else [
                (
                    q - 1, lax.rem(self.plane + q, self.planes),
                    lax.rem(self.plane + q, self.planes),
                )
                for q in range(1, self.planes)
            ]
        near, far = self.order(j, s)
        if second:
            return [(2, flip(self.plane, far), flip(self.plane, far))]
        peer = flip(self.plane, near)
        return [(0, peer, peer), (1, peer, flip(peer, far))]

    def order(self, j, s):
        near = 2 - self.core if self.near else 1 + (j + s + self.core) % 2
        return near, 3 - near

    def copy_c(self, j, s, i, size, at):
        job = self.jobs[j]
        src = job.cut(self.bufs[j][3].at[s], at, size)
        dst = job.cut(self.bufs[j][4].at[s], at, size)
        peer = (self.plane * CORES + self.core, self.owner(s))
        return remote(src, dst, self.sem_c.at[j, s, i, 0], self.sem_c.at[j, s, i, 1], peer)

    def parts(self, j, plane):
        return enumerate(self.jobs[j].parts(self.planes, plane, self.core))

    def a_start(self, j, s):
        self.copy_a(j, s, 1 - self.core).start()
        self.load_a(j, s).start()

    def b_start(self, j, s):
        own, came = self.bufs[j][0], self.bufs[j][1]
        self.load_a(j, s).wait()
        self.copy_a(j, s, self.core).wait_recv()
        at = (s,) + self.jobs[j].index(0, self.jobs[j].halves[self.core])
        own[at] = (own[at].astype(jnp.float32) + came[at].astype(jnp.float32)).astype(own.dtype)
        self.b_send(j, s, False)

    def b_send(self, j, s, second):
        for slot, peer, piece in self.sends(j, s, second):
            for i, (start, size, cond, at) in self.parts(j, piece):
                guarded(
                    cond, lambda: self.copy_b(j, s, slot, peer, i, start, size, at).start()
                )

    def b_next(self, j, s):
        if self.planes != 4:
            return
        job = self.jobs[j]
        own, came = self.bufs[j][0], self.bufs[j][2]
        near, far = self.order(j, s)
        for slot, piece in ((0, self.plane), (1, flip(self.plane, far))):
            for i, (start, size, cond, at) in self.parts(j, piece):
                def add():
                    self.copy_b(
                        j, s, slot, flip(self.plane, near), i, start, size, at
                    ).wait_recv()
                    at_own = (s,) + job.index(start, size)
                    got = came[(s, slot) + job.index(at, size)].astype(jnp.float32)
                    own[at_own] = (own[at_own].astype(jnp.float32) + got).astype(own.dtype)
                guarded(cond, add)
        self.b_send(j, s, True)

    def c_start(self, j, s):
        job = self.jobs[j]
        own, came, piece = self.bufs[j][0], self.bufs[j][2], self.bufs[j][3]
        slots = [2] if self.planes == 4 else range(self.planes - 1)
        for i, (start, size, cond, at) in self.parts(j, self.plane):
            def add():
                total = own[(s,) + job.index(start, size)].astype(jnp.float32)
                for slot in slots:
                    self.copy_b(j, s, slot, self.plane, i, start, size, at).wait_recv()
                    total = total + came[(s, slot) + job.index(at, size)].astype(jnp.float32)
                piece[(s,) + job.index(at, size)] = total.astype(piece.dtype)
                if s < self.shards - 1:
                    self.copy_c(j, s, i, size, at).start()
            guarded(cond, add)

    def total(self, j):
        job = self.jobs[j]
        piece, came = self.bufs[j][3], self.bufs[j][4]
        final = self.shards - 1
        for i, (start, size, cond, at) in self.parts(j, self.plane):
            def add():
                total = piece[(final,) + job.index(at, size)].astype(jnp.float32)
                for s in range(final):
                    self.copy_c(j, s, i, size, at).wait_recv()
                    total = total + came[(s,) + job.index(at, size)].astype(jnp.float32)
                piece[(final,) + job.index(at, size)] = total.astype(piece.dtype)
            guarded(cond, add)
        if self.keep:
            self.copy_f(j).start()

    def copy_f(self, j):
        return pltpu.make_async_copy(
            self.bufs[j][3].at[self.shards - 1], self.fins[j], self.sem_f.at[j]
        )

    def finish(self, j):
        if self.keep:
            self.copy_f(j).wait()
        for s in range(self.shards):
            self.copy_a(j, s, 1 - self.core).wait_send()
            for slot, peer, piece in self.sends(j, s, False) + self.sends(j, s, True):
                for i, (start, size, cond, at) in self.parts(j, piece):
                    guarded(
                        cond,
                        lambda: self.copy_b(j, s, slot, peer, i, start, size, at).wait_send(),
                    )
        for i, (start, size, cond, at) in self.parts(j, self.plane):
            def sent():
                for s in range(self.shards - 1):
                    self.copy_c(j, s, i, size, at).wait_send()
            guarded(cond, sent)


class ReduceHere(Reduce):
    def locate(self, j, s):
        return self.grads[j].at[s] if j == 0 else self.grads[j].at[self.owner(s)]


class Share(Engine):
    def __init__(self, jobs, arrays, source=None):
        self.jobs, self.arrays, self.source = jobs, arrays, source
        planes, _ = sizes()
        count = len(jobs)
        dma = pltpu.SemaphoreType.DMA
        self.outs = [
            jax.ShapeDtypeStruct((job.rows, job.columns), jnp.bfloat16) for job in jobs
        ]
        self.scratch = [dma((count, planes, 2, 2)), dma((count, 2))]
        if source is None:
            self.scratch += [pltpu.VMEM(a.shape, a.dtype) for a in arrays] + [dma((count,))]

    def bind(self, fins, outs, sems):
        if self.source is not None:
            fins = [bufs[3].at[self.source.shards - 1] for bufs in self.source.bufs]
        self.given = fins
        self.fins, self.outs_ref = fins, outs
        self.sem_d, self.sem_e = sems[:2]
        if self.source is None:
            self.fins, self.sem_f = sems[2:-1], sems[-1]
        self.plane, self.core, self.row, self.planes, self.shards = place()

    def parts(self, j, plane):
        return enumerate(self.jobs[j].parts(self.planes, plane, self.core))

    def fetch(self, j):
        return pltpu.make_async_copy(self.given[j], self.fins[j], self.sem_f.at[j])

    def copy_d(self, j, q, i, start, size, at):
        job = self.jobs[j]
        src = job.cut(self.fins[j], at, size)
        dst = job.cut(self.outs_ref[j], start + job.starts[self.core], size)
        sems = self.sem_d.at[j, q, i, 0], self.sem_d.at[j, q, i, 1]
        if q == 0:
            return pltpu.make_async_copy(src, dst, sems[0])
        return remote(
            src, dst, *sems, plane_peer(self.plane, self.core, self.row, self.planes, q)
        )

    def copy_e(self, j, core):
        job = self.jobs[j]
        ref = job.cut(self.outs_ref[j], job.starts[core], job.halves[core])
        peer = (self.plane * CORES + 1 - self.core, self.row)
        return remote(ref, ref, self.sem_e.at[j, 0], self.sem_e.at[j, 1], peer)

    def start(self, j):
        if self.source is None:
            self.fetch(j).wait()
        for i, (start, size, cond, at) in self.parts(j, self.plane):
            def send():
                for q in range(self.planes):
                    self.copy_d(j, q, i, start, size, at).start()
            guarded(cond, send)

    def across(self, j):
        for q in range(1, self.planes):
            origin = lax.rem(self.plane + self.planes - q, self.planes)
            for i, (start, size, cond, at) in self.parts(j, origin):
                guarded(cond, lambda: self.copy_d(j, q, i, start, size, at).wait_recv())
        for i, (start, size, cond, at) in self.parts(j, self.plane):
            guarded(cond, lambda: self.copy_d(j, 0, i, start, size, at).wait())
        self.copy_e(j, self.core).start()

    def finish(self, j):
        self.copy_e(j, 1 - self.core).wait_recv()
        self.copy_e(j, self.core).wait_send()
        for i, (start, size, cond, at) in self.parts(j, self.plane):
            def sent():
                for q in range(1, self.planes):
                    self.copy_d(j, q, i, start, size, at).wait_send()
            guarded(cond, sent)


def any_spec():
    return pl.BlockSpec(memory_space=pl.ANY)


def sizes():
    return lax.axis_size("ctx") // CORES, lax.axis_size("fsdp")


def fused_call(
    kernel, steps, args, in_specs, out_specs, out_shape, scratch, engines, schedule, end, ident,
    chain=False, cost=None,
):
    n_in, n_out, n_scr = len(args), len(out_shape), len(scratch)
    e_in = [len(e.arrays) for e in engines]
    e_out = [len(e.outs) for e in engines]
    e_scr = [len(e.scratch) for e in engines]

    def cut(refs, first, counts):
        groups = [refs[:first]]
        for count in counts:
            groups.append(refs[first : first + count])
            first += count
        return groups, refs[first:]

    def kern(*refs):
        ins, refs = cut(refs, n_in, e_in)
        outs, refs = cut(refs, n_out, e_out)
        scrs, refs = cut(refs, n_scr, e_scr)
        for k, engine in enumerate(engines):
            engine.bind(ins[k + 1], outs[k + 1], scrs[k + 1])
        step = pl.program_id(0)
        pl.when(step == 0)(lambda: greet(chain))
        for when in sorted(schedule):
            def act():
                for action in schedule[when]:
                    action()
            pl.when(step == when)(act)
        if kernel is not None:
            kernel(*ins[0], *outs[0], *scrs[0])
        def close():
            for action in end:
                action()
        pl.when(step == steps - 1)(close)

    flat = lambda groups: [item for group in groups for item in group]
    found = pl.pallas_call(
        kern,
        grid=(steps,),
        in_specs=list(in_specs) + [any_spec()] * sum(e_in),
        out_specs=list(out_specs) + [any_spec()] * sum(e_out),
        out_shape=list(out_shape) + flat([e.outs for e in engines]),
        scratch_shapes=list(scratch) + flat([e.scratch for e in engines]),
        compiler_params=pltpu.CompilerParams(
            vmem_limit_bytes=VMEM_BYTES, collective_id=ident, has_side_effects=True,
            fuse_transposed_lhs_in_matmul=True,
        ),
        cost_estimate=cost,
    )(*args, *flat([e.arrays for e in engines]))
    groups, _ = cut(found, n_out, e_out)
    return groups


def call(action, *given):
    return lambda: action(*given)


class HaloBack:
    def __init__(self, pairs, wide):
        self.arrays = []
        self.pairs = pairs
        dma = pltpu.SemaphoreType.DMA
        self.outs = [jax.ShapeDtypeStruct((2 * pairs, WINDOW, TILE), jnp.bfloat16)]
        self.scratch = [
            pltpu.VMEM((pairs, 2, WINDOW, TILE), jnp.bfloat16), dma((pairs, 2, 2)),
        ]

    def bind(self, _, outs, refs):
        (self.out,), (self.buf, self.sems) = outs, refs
        self.ctx, self.row = lax.axis_index("ctx"), lax.axis_index("fsdp")
        self.last = lax.axis_size("ctx") - 1

    def copy(self, pair, side):
        return remote(
            self.buf.at[pair, side], self.out.at[side * self.pairs + pair],
            self.sems.at[pair, side, 0], self.sems.at[pair, side, 1],
            (jnp.maximum(self.ctx - 1, 0), self.row),
        )

    def send(self, pair):
        @pl.when(self.ctx > 0)
        def _():
            for side in range(2):
                self.copy(pair, side).start()

    def finish(self):
        @pl.when(self.ctx > 0)
        def _():
            for pair in range(self.pairs):
                for side in range(2):
                    self.copy(pair, side).wait_send()

        @pl.when(self.ctx < self.last)
        def _():
            for pair in range(self.pairs):
                for side in range(2):
                    self.copy(pair, side).wait_recv()


class Small:
    def __init__(self, array):
        self.arrays = [array]
        planes, shards = sizes()
        dma = pltpu.SemaphoreType.DMA
        self.outs = [jax.ShapeDtypeStruct(array.shape, jnp.float32)]
        self.peers = 1, planes - 1, shards - 1
        self.scratch = [
            pltpu.VMEM((4,) + array.shape, jnp.float32),
            pltpu.VMEM((sum(self.peers),) + array.shape, jnp.float32),
            dma((sum(self.peers), 2)), dma((2,)),
        ]

    def bind(self, given, outs, refs):
        (self.given,), (self.out,) = given, outs
        self.own, self.came, self.sems, self.sem_l = refs
        self.plane, self.core, self.row, self.planes, self.shards = place()

    def load(self):
        return pltpu.make_async_copy(self.given, self.own.at[0], self.sem_l.at[0])

    def save(self):
        return pltpu.make_async_copy(self.own.at[3], self.out, self.sem_l.at[1])

    def copy(self, stage, n):
        at = sum(self.peers[:stage]) + n
        if stage == 0:
            peer = (self.plane * CORES + 1 - self.core, self.row)
        elif stage == 1:
            peer = plane_peer(self.plane, self.core, self.row, self.planes, n + 1)
        else:
            peer = (self.plane * CORES + self.core, lax.rem(self.row + n + 1, self.shards))
        return remote(
            self.own.at[stage], self.came.at[at], self.sems.at[at, 0], self.sems.at[at, 1], peer
        )

    def send(self, stage):
        for n in range(self.peers[stage]):
            self.copy(stage, n).start()

    def add(self, stage):
        total = self.own[stage]
        for n in range(self.peers[stage]):
            self.copy(stage, n).wait_recv()
            total = total + self.came[sum(self.peers[:stage]) + n]
        self.own[stage + 1] = total

    def finish(self):
        self.save().start()
        for stage in range(3):
            for n in range(self.peers[stage]):
                self.copy(stage, n).wait_send()
        self.save().wait()


def layer_norm(values, gain, shift):
    middle = jnp.mean(values, axis=-1, keepdims=True)
    centred = values - middle
    spread = jnp.mean(centred * centred, axis=-1, keepdims=True)
    return centred * lax.rsqrt(spread + epsilon) * gain + shift


def passed_along(value, axis, by):
    peers = lax.axis_size(axis)
    pairs = [(i, i + by) for i in range(peers) if 0 <= i + by < peers]
    return lax.ppermute(value, axis, pairs)


def segment_ids(lengths_row, positions):
    ends = jnp.cumsum(lengths_row)
    found = jnp.sum((positions[:, None] >= ends[None, :]).astype(jnp.int32), axis=1)
    return jnp.where(positions >= 0, found, -1)


def padded(array, parts):
    rows, columns = array.shape
    each = columns // parts
    wide = -(-each // TILE) * TILE
    array = array.reshape(rows, parts, each)
    return jnp.pad(array, ((0, 0), (0, 0), (0, wide - each))).reshape(rows, parts * wide)


def widened(array, columns):
    return jnp.pad(array, ((0, 0), (0, columns - array.shape[1])))


def even(columns):
    return -(-columns // (CORES * TILE)) * CORES * TILE


def on_device(
    activations, doc_lengths, cotangent, attn_gain, attn_shift, w_qkv, query_bias, value_bias,
    w_out, out_bias, mlp_gain, mlp_shift, w_fc, fc_bias, w_proj, proj_bias,
):
    low = jnp.bfloat16
    shards = lax.axis_size("fsdp")
    shard_rows, hidden = w_fc.shape
    features = activations.shape[2]
    wide = -(-features // TILE) * TILE
    pairs = wide // TILE
    qkv_wide, out_wide = even(3 * wide), even(features)
    own_hidden = w_proj.shape[0]
    first = own_hidden * 8 // 17
    second = own_hidden - first
    job_qkv, job_out = best_job(shard_rows, qkv_wide), best_job(shard_rows, out_wide)
    jobs_a = [best_job(shard_rows, shards * first), Job(0, first, features)]
    jobs_b = [best_job(shard_rows, shards * second), Job(0, second, features)]
    uneven_b = [
        best_job(shard_rows, shards * second, 0.35), Job(0, second, features, 0, 0.35)
    ]

    x_t, cot_t = activations[0].T, cotangent[0].T
    tok = x_t.shape[1]
    vectors = (
        attn_gain, attn_shift, query_bias, value_bias, out_bias, mlp_gain, mlp_shift, proj_bias,
    )
    vec = jnp.concatenate([v[None] for v in vectors] + [fc_bias.reshape(-1, shard_rows)])
    vec = jnp.pad(vec, ((0, 2 * TILE - vec.shape[0]), (0, 0))).T
    (
        qkv, halo, normed1_t, cot, vfull, qkv_w, fc_a, fc_b, proj_a, proj_b, out_low,
    ) = first_call(
        x_t, cot_t, w_qkv, vec, w_fc, w_proj, w_out, first, wide, qkv_wide, out_wide, 0
    )
    qkv_w = qkv_w.reshape(features, qkv_wide)
    vfull = vfull[:, :, :TILE].astype(jnp.float32)
    gain_one = vfull[:, :, 0].reshape(features, 1)
    vec_two = jnp.stack([vfull[:, :, n].reshape(-1) for n in (4, 5, 6, 7)])
    pbias = vec_two[3:4]
    fcbias = vfull[:, :, 8 : 8 + own_hidden // shard_rows].transpose(0, 2, 1)
    fcbias = fcbias.reshape(shards, own_hidden)

    first_pos = lax.axis_index("ctx") * tok
    ext_positions = first_pos - WINDOW + jnp.arange(tok + WINDOW, dtype=jnp.int32)
    doc_ext = segment_ids(doc_lengths[0], ext_positions)
    ids = jnp.arange(TILE, dtype=jnp.int32)[None, :]
    same = doc_ext[:, None] == ids
    qdoc = same[WINDOW:].astype(low)
    kdoc = jnp.where(same | (ids >= doc_lengths.shape[1]), 0.0, masked_score).astype(low)

    (attended, full, stat), (out_w, fc_wa, proj_wa) = attention_forward(
        qkv, halo, qdoc, kdoc, features,
        Gather([job_out] + jobs_a, [out_low, fc_a, proj_a]),
        1,
    )
    out_w = out_w.reshape(features, out_wide)
    lse = stat.T[: 2 * pairs].reshape(pairs, 2, tok)
    resid, normed2_low, normed2_t = out_norm(attended, out_w, x_t, vec_two)
    fcb_a = fcbias[:, :first].reshape(1, -1)
    fcb_b = fcbias[:, first:].reshape(1, -1)
    rest = Gather(jobs_b, [fc_b, proj_b])
    (base, dnorm_a, gproj_a, gfc_a, gfcb_a), (fc_wb, proj_wb) = mlp_part(
        normed2_low, normed2_t, cot, cot_t, resid, None, None,
        fc_wa.reshape(features, -1), fcb_a, proj_wa.reshape(-1, features),
        rest, *gather_plan(rest, shards * first // 256), 2,
    )
    sum_a = Reduce(
        jobs_a,
        [gfc_a.reshape(shards, shard_rows, -1), gproj_a.reshape(shards, first, features)],
    )
    schedule, end, done = reduce_plan(sum_a, shards * second // 256, shards * second // 256 - 3)
    (block_out, dnormed2, gproj_b, gfc_b, gfcb_b), fins_a = mlp_part(
        normed2_low, normed2_t, cot, cot_t, base, dnorm_a, pbias,
        fc_wb.reshape(features, -1), fcb_b, proj_wb.reshape(-1, features),
        sum_a, schedule, end + done, 3,
    )
    gresid_t, grad_attended, grad_wout, mid_sums = middle(
        dnormed2, resid, cot, attended, out_w, vec_two
    )
    sum_b = Reduce(
        uneven_b,
        [gfc_b.reshape(shards, shard_rows, -1), gproj_b.reshape(shards, second, features)],
        near=2,
    )
    (dq, dko, dvo), fins_b, (r_fca, r_proja), (back,) = attention_backward(
        qkv, halo, grad_attended, full, lse, qdoc, kdoc, features, sum_b,
        Share(jobs_a, fins_a), 4,
    )
    small = jnp.concatenate([
        jnp.zeros((4, features), jnp.float32),
        jnp.stack([mid_sums[2], mid_sums[0], mid_sums[1], mid_sums[3]]),
        jnp.concatenate(
            [gfcb_a.reshape(shards, first), gfcb_b.reshape(shards, second)], axis=1
        ).reshape(-1, features),
    ])
    small = jnp.pad(small, ((0, -small.shape[0] % 8), (0, 0)))
    input_grad_t, r_qkv, r_out, r_fcb, r_projb, small = last_call(
        [job_qkv, job_out], Share(uneven_b, fins_b), normed1_t, x_t, gain_one, dq, dko, dvo, back, qkv_w, gresid_t,
        grad_wout.reshape(shards, shard_rows, out_wide), small, 5,
    )
    r_qkv, r_out, r_fc, r_proj = finals(
        features, shards, r_qkv, r_out, r_fca, r_fcb, r_proja, r_projb
    )
    row = lax.axis_index("fsdp")
    sums = [
        lax.dynamic_slice_in_dim(small[n], row * shard_rows, shard_rows) for n in range(8)
    ]
    fcb_sum = lax.dynamic_slice_in_dim(
        small[8 : 8 + hidden // features].reshape(-1), row * own_hidden, own_hidden
    )
    return (
        block_out.T[None], input_grad_t.T[None], sums[0], sums[1], r_qkv, sums[2], sums[3], r_out,
        sums[4], sums[5], sums[6], r_fc, fcb_sum, r_proj, sums[7],
    )


def solution(mesh):
    vec, mat = P("fsdp"), P("fsdp", None)
    seq = P("fsdp", "ctx", None)
    placed = (
        seq, mat, seq, vec, vec, mat, vec, vec, mat, vec, vec, vec, mat, vec, mat, vec,
    )
    return jax.shard_map(
        on_device,
        mesh=mesh,
        in_specs=placed,
        out_specs=(seq, seq, vec, vec, mat, vec, vec, mat, vec, vec, vec, mat, vec, mat, vec),
        check_vma=False,
    )
```

time: 1650 us -> 618 us (0.37)
  waiting for transfers between devices: 736 us -> 0 us
  Pallas kernels: 0 us -> 576 us
  matrix products: 524 us -> 0 us
  other arithmetic: 178 us -> 5.52 us
  blocking collectives: 75.8 us -> 0 us
  local copies, waits for them, and re-layouts: 95.7 us -> 26.6 us
  between operations: 17.8 us -> 1.12 us
    pallas_call x0 -> x9, Pallas kernels: none -> 576 us  [the longest x4 342 us: fused_call(): pl.pallas_call(kern, grid=(steps,), in_specs=list(in_specs) + [any_spec()...]
    dot_general x26 -> x0, matrix products: 524 us -> none  [the longest x4 86.9 us: block_scores(): jnp.einsum('qhe,khe->hqk', query_block, key_block, preferred_element_type...]
    all_gather x7 -> x0, waiting for transfers between devices: 306 us -> none  [the longest x1 156 us: gather_first(): lax.all_gather(lows[11], 'fsdp', axis=0, tiled=True)]
    unnamed x21 -> x0, waiting for transfers between devices: 266 us -> none
    reduce_scatter x2 -> x0, waiting for transfers between devices: 162 us -> none  [the longest x1 81.7 us: on_device(): lax.psum_scatter(grad_wproj.astype(jnp.bfloat16), 'ctx', scatter_dimensio...]
    convert_element_type x24 -> x3, other arithmetic: 103 us -> 2.91 us  [the longest x1 1.15 us: on_device(): jnp.where(same | (ids >= doc_lengths.shape[1]), 0.0, masked_score)]
    reduce_sum x10 -> x0, other arithmetic: 60.7 us -> none  [the longest x2 47.4 us: forward_block(): row_total = jnp.sum(expo, axis=-1, keepdims=True)]
    unnamed x2 -> x0, blocking collectives: 37.5 us -> none
  transfers between devices with their start and end apart: 17 -> 0, of which waited for: 14 -> 0; matrix products, arithmetic and copies ran while one was open for 22% -> 0% of each run, Pallas kernels for 0% -> 0%
where the time goes in v1:
time: 618 us; the launch traced here: 609 us
  Pallas kernels  576 us (93%)
  local copies, waits for them, and re-layouts  26.6 us (4%)
    pallas_call x4, Pallas kernels, fused_call(): pl.pallas_call(kern, grid=(steps,), in_specs=list(in_specs) + [any_spec()...  342 us
    pallas_call x1, Pallas kernels, last_call(): pl.pallas_call(lambda *refs: last_kernel(reduce, early, late, tiny, (feat...  118 us
    pallas_call x1, Pallas kernels, first_call(): pl.pallas_call(lambda *refs: first_kernel(engine, dims, *refs), in_specs=...  80.6 us
    pallas_call x1, Pallas kernels, middle(): pl.pallas_call(lambda *refs: middle_kernel(steps, *refs), grid=(steps,),...  17.4 us

profile of v1, /device:TPU:7, one launch (start us, length us, event | category | flops | bytes accessed | tf_op | source)
XLA Modules:
  0.0 609.0 jit_solution(7478867360129337765)
XLA Ops:
  0.7 0.8 reduce-window.8
  4.2 0.7 broadcast_in_dim.53
  7.0 0.8 reshape.137
  8.0 0.7 pad_bitcast_fusion.refs_3_
  9.1 0.8 slice_convert_fusion.refs_5_.refs_8_
  9.8 1.2 select_convert_fusion.refs_6_.refs_9_
  11.0 80.6 %shard_map.271 = (bf16[1024,3584]{1,0:T(8,128)(2,1)}, bf16[1024,2304]{1,0:T(8,128)(2,1)}, bf16[1088,1024]{1,0:T(8,128)(2,1)}, bf16[1024,1088]{1,0:T(8,128)(2,1)}...) custom-call(bf16[1088,1024]{1,0:T(8,128)(2,1)} %bitcast.37, ...), custom_call_target="tpu_custom_call" | custom-call | tf_op jit(solution)/shard_map/pallas_call | solution.py:799
  91.6 1.0 slice_convert_fusion.1
  93.2 0.7 reshape.146.refs_8_
  94.5 2.2 slice_reduce_fusion.3
  97.7 69.8 %shard_map.272 = (bf16[1024,1088]{1,0:T(8,128)(2,1)}, f32[1024,1152]{1,0:T(8,128)}, f32[1024,128]{1,0:T(8,128)}, bf16[4,272,1280]{2,1,0:T(8,128)(2,1)}, bf16[4,2...) custom-call(bf16[1024,3584]{1,0:T(8,128)(2,1)} %get-tuple-element.71.refs_0_.refs_2_.refs_4_, ...), custom_call_target="tpu_custom_call" | custom-call | flops 22817013760 | bytes 22282240 | tf_op jit(solution)/shard_map/pallas_call | solution.py:1606
  167.6 1.2 copy.48
  168.8 0.7 reshape.151.refs_7_
  169.5 9.5 %shard_map.273 = (f32[1024,1088]{1,0:T(8,128)}, bf16[1024,1088]{1,0:T(8,128)(2,1)}, bf16[1088,1024]{1,0:T(8,128)(2,1)}) custom-call(bf16[1024,1088]{1,0:T(8,128)(2,1)} %get-tuple-element.76.att_ref.refs_3_, bf16[1088,1280]{1,0:T(8,128)(2,1)} %bitcast.40, bf16[1088,1024]{1,0:T(8,128)(2,1)} %bitcast.38, f32[4,1088]{1,0:T(4,128)} %pad_maximum_fusion.vec_ref.refs_5_), custom_call_target="tpu_custom_call" | custom-call | tf_op jit(solution)/shard_map/pallas_call | solution.py:900
  179.0 76.5 %shard_map.274 = (f32[1024,1088]{1,0:T(8,128)}, f32[1024,1088]{1,0:T(8,128)}, bf16[2048,1088]{1,0:T(8,128)(2,1)}, bf16[1088,2048]{1,0:T(8,128)(2,1)}, f32[1,2048...) custom-call(bf16[1024,1088]{1,0:T(8,128)(2,1)} %get-tuple-element.79.refs_0_, ...), custom_call_target="tpu_custom_call" | custom-call | flops 27380416512 | bytes 40108032 | tf_op jit(solution)/shard_map/pallas_call | solution.py:1606
  255.6 74.2 %shard_map.275 = (bf16[1088,1024]{1,0:T(8,128)(2,1)}, f32[1024,1088]{1,0:T(8,128)}, bf16[2304,1088]{1,0:T(8,128)(2,1)}, bf16[1088,2304]{1,0:T(8,128)(2,1)}, f32[...) custom-call(bf16[1024,1088]{1,0:T(8,128)(2,1)} %get-tuple-element.79.refs_0_, ...), custom_call_target="tpu_custom_call" | custom-call | flops 30802968576 | bytes 42336256 | tf_op jit(solution)/shard_map/pallas_call | solution.py:1606
  329.8 17.4 %shard_map.276 = (f32[1088,1024]{1,0:T(8,128)}, bf16[1024,1088]{1,0:T(8,128)(2,1)}, bf16[1088,1280]{1,0:T(8,128)(2,1)}, f32[8,1088]{1,0:T(8,128)}) custom-call(f32[1024,1088]{1,0:T(8,128)} %get-tuple-element.95.refs_0_, f32[1024,1088]{1,0:T(8,128)} %get-tuple-element.82.refs_4_.refs_1_, bf16[1024,1088]{1,0:T(8,128)(2,1)} %get-tuple-element.81.refs_2_, ...), custom_call_target="tpu_custom_call" | custom-call | tf_op jit(solution)/shard_map/pallas_call | solution.py:959
  347.2 121.4 %shard_map.277 = (bf16[1024,1152]{1,0:T(8,128)(2,1)}, bf16[1024,1152]{1,0:T(8,128)(2,1)}, bf16[1024,1152]{1,0:T(8,128)(2,1)}, bf16[48,2304]{1,0:T(8,128)(2,1)}, ...) custom-call(bf16[1024,3584]{1,0:T(8,128)(2,1)} %get-tuple-element.71, ...), custom_call_target="tpu_custom_call" | custom-call | flops 57042534400 | bytes 44564480 | tf_op jit(solution)/shard_map/pallas_call | solution.py:1606
  470.7 117.7 %shard_map.278 = (f32[1088,1024]{1,0:T(8,128)}, bf16[272,3584]{1,0:T(8,128)(2,1)}, bf16[272,1280]{1,0:T(8,128)(2,1)}, bf16[272,2304]{1,0:T(8,128)(2,1)}, bf16[576,1088]{1,0:T(8,128)(2,1)}, /*index=5*/f32[16,1088]{1,0:T(8,128)}) custom-call(bf16[4,272,1024]{2,1,0:T(8,128)(2,1)} %bitcast.49, bf16[1088,1024]{1,0:T(8,128)(2,1)} %bitcast.39, f32[1088,1]{1,0:T(8,128)} %bitcast.45, ...), custom_call_target="tpu_custom_call" | custom-call | tf_op jit(solution)/shard_map/pallas_call | solution.py:508
  588.4 0.8 slice.92
  589.2 1.2 fusion.8
  593.9 8.5 %shard_map.279 = (f32[272,3264]{1,0:T(8,128)}, f32[272,1088]{1,0:T(8,128)}, f32[272,4352]{1,0:T(8,128)}, f32[1088,1088]{1,0:T(8,128)}) custom-call(bf16[272,3584]{1,0:T(8,128)(2,1)} %get-tuple-element.117.refs_0_, bf16[272,1280]{1,0:T(8,128)(2,1)} %get-tuple-element.118.refs_1_, bf16[272,2048]{1,0:T(8,128)(2,1)} %get-tuple-element.119.refs_2_, ...), custom_call_target="tpu_custom_call" | custom-call | tf_op jit(solution)/shard_map/pallas_call | solution.py:871
  602.4 1.4 copy.52
  603.7 5.0 copy.53
  (52 shorter events, 13.0 us)
Async XLA Ops:
  96.9 70.6 %copy-start.1 = (f32[1,1088]{1,0:T(1,128)}, f32[1,1088]{1,0:T(1,128)S(1)}, u32[]{:S(2)}) copy-start(f32[1,1088]{1,0:T(1,128)S(1)} %stack_reshape_squeeze.15.refs_6_) | copy-start | bytes 13060
  347.2 122.0 %copy-start.4 = (f32[1,2048]{1,0:T(1,128)S(1)}, f32[1,2048]{1,0:T(1,128)}, u32[]{:S(2)}) copy-start(f32[1,2048]{1,0:T(1,128)} %get-tuple-element.113) | copy-start | bytes 24580
  347.2 122.7 %copy-start.2 = (f32[8,1088]{1,0:T(8,128)S(1)}, f32[8,1088]{1,0:T(8,128)}, u32[]{:S(2)}) copy-start(f32[8,1088]{1,0:T(8,128)} %get-tuple-element.112) | copy-start | bytes 104452
  347.2 122.7 %copy-start.3 = (f32[1,2304]{1,0:T(1,128)S(1)}, f32[1,2304]{1,0:T(1,128)}, u32[]{:S(2)}) copy-start(f32[1,2304]{1,0:T(1,128)} %get-tuple-element.114) | copy-start | bytes 27652
  593.9 8.5 %copy-start = (bf16[1088,1024]{1,0:T(8,128)(2,1)S(1)}, bf16[1088,1024]{1,0:T(8,128)(2,1)}, u32[]{:S(2)}) copy-start(bf16[1088,1024]{1,0:T(8,128)(2,1)} %get-tuple-element.93) | copy-start | bytes 6684676

commit v2 on v1

--- a/solution.py
+++ b/solution.py
@@ -198,7 +198,7 @@
 
 
 def attention_backward(
-    qkv, halo, upstream, full, lse, qdoc, kdoc, features, reduce, share, ident
+    qkv, halo, upstream, full, lse, qdoc, kdoc, features, reduce, ident
 ):
     tok = qkv.shape[0]
     pairs = -(-features // TILE)
@@ -210,11 +210,7 @@
     wide = pairs * TILE
     back = HaloBack(pairs, wide)
     schedule, end, done = reduce_plan(reduce, pairs, pairs - 3)
-    those = range(len(share.jobs))
-    schedule[3] += [call(lambda j: share.fetch(j).start(), j) for j in those]
-    schedule[4] += [share.both(share.start, j) for j in those]
-    schedule[7] += [share.both(share.across, j) for j in those]
-    end += done + [share.both(share.finish, j) for j in those] + [back.finish]
+    end += done + [back.finish]
     return fused_call(
         lambda *refs: attention_backward_kernel(last, tok, back, *refs),
         pairs,
@@ -237,7 +233,7 @@
             pltpu.VMEM((tok + WINDOW, TILE), jnp.float32),
             pltpu.VMEM((8, tok), jnp.float32),
         ],
-        [reduce, share, back],
+        [reduce, back],
         schedule,
         end,
         ident,
@@ -297,8 +293,10 @@
                 out_ref[:, at : at + ROWS] = done.T.astype(jnp.bfloat16)
 
 
-def mlp_part(norm, norm_t, cot, cot_t, base, dbase, pbias, fc_w, fcb, proj_w, engine, schedule, end, ident):
-    tok, features = norm.shape
+def mlp_part(
+    norm, norm_t, cot, cot_t, base, dbase, pbias, fc_w, fcb, proj_w, engine, schedule, end, ident
+):
+    tok, features = cot.shape
     hidden = fc_w.shape[1]
     width = 256
     steps = hidden // width
@@ -306,36 +304,50 @@
     whole = lambda shape: pl.BlockSpec(shape, lambda j: (0, 0), pipeline_mode=pl.Buffered(1))
     cols = lambda rows: pl.BlockSpec((rows, width), lambda j: (0, j))
     rows = pl.BlockSpec((width, features), lambda j: (j, 0))
+    struct = jax.ShapeDtypeStruct
 
     def kern(*refs):
         refs = list(refs)
-        if opening:
-            refs.insert(5, None)
-            refs.insert(6, None)
-            refs.insert(15, refs[10])
-        mlp_kernel(steps, opening, *refs)
-
+        if not opening:
+            mlp_kernel(steps, False, *refs)
+            return
+        att, w, xt, vec, cot_ref, cott_ref, fc, fcb_ref, proj = refs[:9]
+        out, dnorm, gproj, gfc, gfcb, resid, norm_ref, normt_ref = refs[9:17]
+
+        @pl.when(pl.program_id(0) == 0)
+        def _():
+            out_norm(att, w, xt, vec, resid, norm_ref, normt_ref)
+
+        mlp_kernel(
+            steps, True, norm_ref, normt_ref, cot_ref, cott_ref, resid, None, None, fc, fcb_ref,
+            proj, out, dnorm, gproj, gfc, gfcb, out, *refs[17:]
+        )
+
+    if opening:
+        attended, out_w, x_t, vec = norm
+        args = (attended, out_w, x_t, vec, cot, cot_t, fc_w, fcb, proj_w)
+    else:
+        args = (norm, norm_t, cot, cot_t, base, dbase, pbias, fc_w, fcb, proj_w)
     extra = [] if opening else [pltpu.VMEM((tok, features), jnp.float32)]
+    more = [
+        struct((tok, features), jnp.float32), struct((tok, features), jnp.bfloat16),
+        struct((features, tok), jnp.bfloat16),
+    ] if opening else []
     return fused_call(
         kern,
         steps,
-        (norm, norm_t, cot, cot_t, base) + (() if opening else (dbase, pbias)) + (fc_w, fcb, proj_w),
-        [whole((tok, features)), whole((features, tok))] * 2
-        + [whole((tok, features))] * (1 if opening else 2)
-        + ([] if opening else [whole((1, features))])
-        + [cols(features), cols(1), rows],
+        args,
+        [whole(a.shape) for a in args[:-3]] + [cols(features), cols(1), rows],
         [
             whole((tok, features) if opening else (features, tok)), whole((tok, features)), rows,
             cols(features), cols(1),
-        ],
+        ] + [whole(a.shape) for a in more],
         [
-            jax.ShapeDtypeStruct((tok, features), jnp.float32)
-            if opening else jax.ShapeDtypeStruct((features, tok), jnp.bfloat16),
-            jax.ShapeDtypeStruct((tok, features), jnp.float32),
-            jax.ShapeDtypeStruct((hidden, features), jnp.bfloat16),
-            jax.ShapeDtypeStruct((features, hidden), jnp.bfloat16),
-            jax.ShapeDtypeStruct((1, hidden), jnp.float32),
-        ],
+            struct((tok, features), jnp.float32)
+            if opening else struct((features, tok), jnp.bfloat16),
+            struct((tok, features), jnp.float32), struct((hidden, features), jnp.bfloat16),
+            struct((features, hidden), jnp.bfloat16), struct((1, hidden), jnp.float32),
+        ] + more,
         extra
         + [pltpu.VMEM((tok, width), jnp.bfloat16), pltpu.VMEM((tok, width), jnp.bfloat16)],
         [engine],
@@ -829,10 +841,12 @@
 
 
 def final_kernel(
-    features, shards, qkv_ref, out_ref, fca_ref, fcb_ref, pa_ref, pb_ref,
-    gqkv_ref, gout_ref, gfc_ref, gproj_ref,
+    features, shards, qkv_ref, out_ref, fca_ref, fcb_ref, block_ref, input_ref, pa_ref, pb_ref,
+    gqkv_ref, gout_ref, gfc_ref, block_out, input_out, gproj_ref,
 ):
     step = pl.program_id(0)
+    block_out[...] = block_ref[...]
+    input_out[...] = input_ref[...]
     wide = -(-features // TILE) * TILE
     for n in range(3):
         gqkv_ref[:, n * features : (n + 1) * features] = qkv_ref[
@@ -862,52 +876,40 @@
         pl.when(step == at)(call(proj, at))
 
 
-def finals(features, shards, r_qkv, r_out, r_fca, r_fcb, r_proja, r_projb):
+def finals(
+    features, shards, r_qkv, r_out, r_fca, r_fcb, block_out, input_grad, r_proja, r_projb
+):
     rows, own = r_qkv.shape[0], r_proja.shape[0] + r_projb.shape[0]
     steps = 2 if rows // 2 % 8 == 0 else 1
-    blk = lambda a: pl.BlockSpec((rows // steps, a.shape[1]), lambda i: (i, 0))
+    blk = lambda a: pl.BlockSpec((a.shape[0] // steps, a.shape[1]), lambda i: (i, 0))
     whole = lambda a: pl.BlockSpec(a.shape, lambda i: (0, 0), pipeline_mode=pl.Buffered(1))
+    struct = jax.ShapeDtypeStruct
     shapes = [(rows, 3 * features), (rows, features), (rows, own * shards), (own, features)]
+    shapes = [struct(s, jnp.float32) for s in shapes]
+    shapes[3:3] = [struct(a.shape, a.dtype) for a in (block_out, input_grad)]
     return pl.pallas_call(
         lambda *refs: final_kernel(features, shards, *refs),
         grid=(steps,),
-        in_specs=[blk(a) for a in (r_qkv, r_out, r_fca, r_fcb)]
+        in_specs=[blk(a) for a in (r_qkv, r_out, r_fca, r_fcb, block_out, input_grad)]
         + [whole(r_proja), whole(r_projb)],
-        out_specs=[pl.BlockSpec((s[0] // steps, s[1]), lambda i: (i, 0)) for s in shapes],
-        out_shape=[jax.ShapeDtypeStruct(s, jnp.float32) for s in shapes],
+        out_specs=[blk(s) for s in shapes],
+        out_shape=shapes,
         compiler_params=pltpu.CompilerParams(vmem_limit_bytes=VMEM_BYTES),
-    )(r_qkv, r_out, r_fca, r_fcb, r_proja, r_projb)
-
-
-def out_norm_kernel(att_ref, w_ref, xt_ref, vec_ref, resid_ref, norm_ref, normt_ref):
-    features = resid_ref.shape[1]
-    mixed = dot_f32(att_ref[...], w_ref[...])[:, :features] + vec_ref[0:1]
-    resid = xt_ref[...].astype(jnp.float32).T + mixed
-    resid_ref[...] = resid
-    centred = resid - jnp.mean(resid, axis=1, keepdims=True)
-    spread = jnp.mean(centred * centred, axis=1, keepdims=True)
-    normed = centred * lax.rsqrt(spread + epsilon) * vec_ref[1:2] + vec_ref[2:3]
-    norm_ref[...] = normed.astype(jnp.bfloat16)
-    normt_ref[...] = normed.T.astype(jnp.bfloat16)
-
-
-def out_norm(attended, out_w, x_t, vec):
-    tok, features = attended.shape
-    blk = pl.BlockSpec((ROWS, features), lambda i: (i, 0))
-    blk_t = pl.BlockSpec((features, ROWS), lambda i: (0, i))
-    whole = lambda a: pl.BlockSpec(a.shape, lambda i: (0, 0), pipeline_mode=pl.Buffered(1))
-    struct = jax.ShapeDtypeStruct
-    return pl.pallas_call(
-        out_norm_kernel,
-        grid=(tok // ROWS,),
-        in_specs=[blk, whole(out_w), blk_t, whole(vec)],
-        out_specs=[blk, blk, blk_t],
-        out_shape=[
-            struct((tok, features), jnp.float32), struct((tok, features), jnp.bfloat16),
-            struct((features, tok), jnp.bfloat16),
-        ],
-        compiler_params=pltpu.CompilerParams(vmem_limit_bytes=VMEM_BYTES),
-    )(attended, out_w, x_t, vec)
+    )(r_qkv, r_out, r_fca, r_fcb, block_out, input_grad, r_proja, r_projb)
+
+
+def out_norm(att_ref, w_ref, xt_ref, vec_ref, resid_ref, norm_ref, normt_ref):
+    tok, features = resid_ref.shape
+    for at in range(0, tok, ROWS):
+        rows = pl.ds(at, ROWS)
+        mixed = dot_f32(att_ref[rows, :], w_ref[...])[:, :features] + vec_ref[0:1]
+        resid = xt_ref[:, rows].astype(jnp.float32).T + mixed
+        resid_ref[rows, :] = resid
+        centred = resid - jnp.mean(resid, axis=1, keepdims=True)
+        spread = jnp.mean(centred * centred, axis=1, keepdims=True)
+        normed = centred * lax.rsqrt(spread + epsilon) * vec_ref[1:2] + vec_ref[2:3]
+        norm_ref[rows, :] = normed.astype(jnp.bfloat16)
+        normt_ref[:, rows] = normed.T.astype(jnp.bfloat16)
 
 
 def middle_kernel(
@@ -949,27 +951,35 @@
             gout_ref[:, some] = grad.T.astype(jnp.bfloat16)
 
 
-def middle(dnorm, resid, cot, attended, out_w, vec):
+def middle(dnorm, resid, cot, attended, out_w, vec, share, ident):
     tok, features = resid.shape
     steps = tok // ROWS
     blk = pl.BlockSpec((ROWS, features), lambda i: (i, 0))
     blk_t = pl.BlockSpec((features, ROWS), lambda i: (0, i))
     whole = lambda shape: pl.BlockSpec(shape, lambda i: (0, 0), pipeline_mode=pl.Buffered(1))
     struct = jax.ShapeDtypeStruct
-    return pl.pallas_call(
+    those = range(len(share.jobs))
+    schedule = {
+        0: [call(lambda j: share.fetch(j).start(), j) for j in those],
+        1: [share.both(share.start, j) for j in those],
+        3: [share.both(share.across, j) for j in those],
+    }
+    return fused_call(
         lambda *refs: middle_kernel(steps, *refs),
-        grid=(steps,),
-        in_specs=[blk, blk, blk, whole(attended.shape), whole(out_w.shape), whole(vec.shape)],
-        out_specs=[blk_t, blk, whole(out_w.shape), whole((8, features))],
-        out_shape=[
+        steps,
+        (dnorm, resid, cot, attended, out_w, vec),
+        [blk, blk, blk, whole(attended.shape), whole(out_w.shape), whole(vec.shape)],
+        [blk_t, blk, whole(out_w.shape), whole((8, features))],
+        [
             struct((features, tok), jnp.float32), struct((tok, features), jnp.bfloat16),
             struct(out_w.shape, jnp.bfloat16), struct((8, features), jnp.float32),
         ],
-        scratch_shapes=[pltpu.VMEM((features, tok), jnp.bfloat16)],
-        compiler_params=pltpu.CompilerParams(
-            vmem_limit_bytes=VMEM_BYTES, fuse_transposed_lhs_in_matmul=True
-        ),
-    )(dnorm, resid, cot, attended, out_w, vec)
+        [pltpu.VMEM((features, tok), jnp.bfloat16)],
+        [share],
+        schedule,
+        [share.both(share.finish, j) for j in those],
+        ident,
+    )
 
 
 MESH = pl.DeviceIdType.MESH
@@ -1812,12 +1822,13 @@
     )
     out_w = out_w.reshape(features, out_wide)
     lse = stat.T[: 2 * pairs].reshape(pairs, 2, tok)
-    resid, normed2_low, normed2_t = out_norm(attended, out_w, x_t, vec_two)
     fcb_a = fcbias[:, :first].reshape(1, -1)
     fcb_b = fcbias[:, first:].reshape(1, -1)
     rest = Gather(jobs_b, [fc_b, proj_b])
-    (base, dnorm_a, gproj_a, gfc_a, gfcb_a), (fc_wb, proj_wb) = mlp_part(
-        normed2_low, normed2_t, cot, cot_t, resid, None, None,
+    (
+        (base, dnorm_a, gproj_a, gfc_a, gfcb_a, resid, normed2_low, normed2_t), (fc_wb, proj_wb),
+    ) = mlp_part(
+        (attended, out_w, x_t, vec_two), None, cot, cot_t, None, None, None,
         fc_wa.reshape(features, -1), fcb_a, proj_wa.reshape(-1, features),
         rest, *gather_plan(rest, shards * first // 256), 2,
     )
@@ -1831,17 +1842,16 @@
         fc_wb.reshape(features, -1), fcb_b, proj_wb.reshape(-1, features),
         sum_a, schedule, end + done, 3,
     )
-    gresid_t, grad_attended, grad_wout, mid_sums = middle(
-        dnormed2, resid, cot, attended, out_w, vec_two
+    (gresid_t, grad_attended, grad_wout, mid_sums), (r_fca, r_proja) = middle(
+        dnormed2, resid, cot, attended, out_w, vec_two, Share(jobs_a, fins_a), 6
     )
     sum_b = Reduce(
         uneven_b,
         [gfc_b.reshape(shards, shard_rows, -1), gproj_b.reshape(shards, second, features)],
         near=2,
     )
-    (dq, dko, dvo), fins_b, (r_fca, r_proja), (back,) = attention_backward(
-        qkv, halo, grad_attended, full, lse, qdoc, kdoc, features, sum_b,
-        Share(jobs_a, fins_a), 4,
+    (dq, dko, dvo), fins_b, (back,) = attention_backward(
+        qkv, halo, grad_attended, full, lse, qdoc, kdoc, features, sum_b, 4
     )
     small = jnp.concatenate([
         jnp.zeros((4, features), jnp.float32),
@@ -1855,8 +1865,8 @@
         [job_qkv, job_out], Share(uneven_b, fins_b), normed1_t, x_t, gain_one, dq, dko, dvo, back, qkv_w, gresid_t,
         grad_wout.reshape(shards, shard_rows, out_wide), small, 5,
     )
-    r_qkv, r_out, r_fc, r_proj = finals(
-        features, shards, r_qkv, r_out, r_fca, r_fcb, r_proja, r_projb
+    r_qkv, r_out, r_fc, block_out, input_grad_t, r_proj = finals(
+        features, shards, r_qkv, r_out, r_fca, r_fcb, block_out, input_grad_t, r_proja, r_projb
     )
     row = lax.axis_index("fsdp")
     sums = [

time: 618 us -> 605 us (0.979)
  Pallas kernels: 576 us -> 569 us
  local copies, waits for them, and re-layouts: 26.6 us -> 20.3 us
    pallas_call x2 -> x0, Pallas kernels: 26.9 us -> none  [the longest x1 17.4 us: middle(): pl.pallas_call(lambda *refs: middle_kernel(steps, *refs), grid=(steps,),...]
    pallas_call x4 -> x5, Pallas kernels: 342 us -> 362 us  [fused_call(): pl.pallas_call(kern, grid=(steps,), in_specs=list(in_specs) + [any_spec()...]
    unnamed x14 -> x10, local copies, waits for them, and re-layouts: 7.01 us -> 0.63 us
where the time goes in v2:
time: 605 us; the launch traced here: 596 us
  Pallas kernels  569 us (94%)
  local copies, waits for them, and re-layouts  20.3 us (3%)
    pallas_call x5, Pallas kernels, fused_call(): pl.pallas_call(kern, grid=(steps,), in_specs=list(in_specs) + [any_spec()...  362 us
    pallas_call x1, Pallas kernels, last_call(): pl.pallas_call(lambda *refs: last_kernel(reduce, early, late, tiny, (feat...  114 us
    pallas_call x1, Pallas kernels, first_call(): pl.pallas_call(lambda *refs: first_kernel(engine, dims, *refs), in_specs=...  80.6 us

profile of v2, /device:TPU:7, one launch (start us, length us, event | category | flops | bytes accessed | tf_op | source)
XLA Modules:
  0.0 595.9 jit_solution(12254162999267552105)
XLA Ops:
  0.7 0.8 reduce-window.8
  4.2 0.7 broadcast_in_dim.53
  4.9 0.7 broadcast_in_dim.54
  5.6 0.7 broadcast_in_dim.55
  6.3 0.7 broadcast_in_dim.56
  7.0 0.8 reshape.137
  8.0 0.7 pad_bitcast_fusion.refs_3_
  9.1 0.8 slice_convert_fusion.refs_5_.refs_8_
  9.8 1.1 select_convert_fusion.refs_6_.refs_9_
  11.0 80.6 %shard_map.271 = (bf16[1024,3584]{1,0:T(8,128)(2,1)}, bf16[1024,2304]{1,0:T(8,128)(2,1)}, bf16[1088,1024]{1,0:T(8,128)(2,1)}, bf16[1024,1088]{1,0:T(8,128)(2,1)}...) custom-call(bf16[1088,1024]{1,0:T(8,128)(2,1)} %bitcast.37, ...), custom_call_target="tpu_custom_call" | custom-call | tf_op jit(solution)/shard_map/pallas_call | solution.py:811
  91.5 1.0 slice_convert_fusion.1
  93.1 0.7 reshape.147.refs_8_
  94.4 2.2 slice_reduce_fusion.3
  97.7 69.7 %shard_map.272 = (bf16[1024,1088]{1,0:T(8,128)(2,1)}, f32[1024,1152]{1,0:T(8,128)}, f32[1024,128]{1,0:T(8,128)}, bf16[4,272,1280]{2,1,0:T(8,128)(2,1)}, bf16[4,2...) custom-call(bf16[1024,3584]{1,0:T(8,128)(2,1)} %get-tuple-element.75.refs_0_.refs_2_.refs_4_, ...), custom_call_target="tpu_custom_call" | custom-call | flops 22817013760 | bytes 22282240 | tf_op jit(solution)/shard_map/pallas_call | solution.py:1616
  167.4 1.2 copy.48
  168.6 0.7 reshape.151.refs_7_
  169.3 78.0 %shard_map.273 = (f32[1024,1088]{1,0:T(8,128)}, f32[1024,1088]{1,0:T(8,128)}, bf16[2048,1088]{1,0:T(8,128)(2,1)}, bf16[1088,2048]{1,0:T(8,128)(2,1)}, f32[1,2048...) custom-call(bf16[1024,1088]{1,0:T(8,128)(2,1)} %get-tuple-element.80, ...), custom_call_target="tpu_custom_call" | custom-call | flops 27380416512 | bytes 40108032 | tf_op jit(solution)/shard_map/pallas_call | solution.py:1616
  247.2 73.1 %shard_map.274 = (bf16[1088,1024]{1,0:T(8,128)(2,1)}, f32[1024,1088]{1,0:T(8,128)}, bf16[2304,1088]{1,0:T(8,128)(2,1)}, bf16[1088,2304]{1,0:T(8,128)(2,1)}, f32[...) custom-call(bf16[1024,1088]{1,0:T(8,128)(2,1)} %get-tuple-element.87.refs_0_, ...), custom_call_target="tpu_custom_call" | custom-call | flops 30802968576 | bytes 42336256 | tf_op jit(solution)/shard_map/pallas_call | solution.py:1616
  320.3 31.9 %shard_map.275 = (f32[1088,1024]{1,0:T(8,128)}, bf16[1024,1088]{1,0:T(8,128)(2,1)}, bf16[1088,1280]{1,0:T(8,128)(2,1)}, f32[8,1088]{1,0:T(8,128)}, bf16[272,2048]{1,0:T(8,128)(2,1)}, /*index=5*/bf16[512,1088]{1,0:T(8,128)(2,1)}) custom-call(f32[1024,1088]{1,0:T(8,128)} %get-tuple-element.95.refs_0_, f32[1024,1088]{1,0:T(8,128)} %get-tuple-element.96.refs_1_, ...), custom_call_target="tpu_custom_call" | custom-call | tf_op jit(solution)/shard_map/pallas_call | solution.py:1616
  352.3 109.7 %shard_map.276 = (bf16[1024,1152]{1,0:T(8,128)(2,1)}, bf16[1024,1152]{1,0:T(8,128)(2,1)}, bf16[1024,1152]{1,0:T(8,128)(2,1)}, bf16[48,2304]{1,0:T(8,128)(2,1)}, ...) custom-call(bf16[1024,3584]{1,0:T(8,128)(2,1)} %get-tuple-element.75.refs_0_.refs_2_.refs_4_, ...), custom_call_target="tpu_custom_call" | custom-call | flops 57042534400 | bytes 44564480 | tf_op jit(solution)/shard_map/pallas_call | solution.py:1616
  464.1 114.3 %shard_map.277 = (f32[1088,1024]{1,0:T(8,128)}, bf16[272,3584]{1,0:T(8,128)(2,1)}, bf16[272,1280]{1,0:T(8,128)(2,1)}, bf16[272,2304]{1,0:T(8,128)(2,1)}, bf16[576,1088]{1,0:T(8,128)(2,1)}, /*index=5*/f32[16,1088]{1,0:T(8,128)}) custom-call(bf16[4,272,1024]{2,1,0:T(8,128)(2,1)} %bitcast.48, bf16[1088,1024]{1,0:T(8,128)(2,1)} %bitcast.39, f32[1088,1]{1,0:T(8,128)} %bitcast.44, ...), custom_call_target="tpu_custom_call" | custom-call | tf_op jit(solution)/shard_map/pallas_call | solution.py:520
  578.4 0.8 slice.92
  579.2 1.2 fusion.8
  583.9 11.8 %shard_map.278 = (f32[272,3264]{1,0:T(8,128)}, f32[272,1088]{1,0:T(8,128)}, f32[272,4352]{1,0:T(8,128)}, bf16[1088,1024]{1,0:T(8,128)(2,1)}, f32[1088,1024]{1,0:T(8,128)}, /*index=5*/f32[1088,1088]{1,0:T(8,128)}) custom-call(bf16[272,3584]{1,0:T(8,128)(2,1)} %get-tuple-element.116.refs_0_, bf16[272,1280]{1,0:T(8,128)(2,1)} %get-tuple-element.117.refs_1_, ...), custom_call_target="tpu_custom_call" | custom-call | tf_op jit(solution)/shard_map/pallas_call | solution.py:890
  (47 shorter events, 11.0 us)
Async XLA Ops:
  96.8 70.5 %copy-start = (f32[1,1088]{1,0:T(1,128)}, f32[1,1088]{1,0:T(1,128)S(1)}, u32[]{:S(2)}) copy-start(f32[1,1088]{1,0:T(1,128)S(1)} %stack_reshape_squeeze.15.refs_6_) | copy-start | bytes 13060
  352.3 110.3 %copy-start.3 = (f32[1,2048]{1,0:T(1,128)S(1)}, f32[1,2048]{1,0:T(1,128)}, u32[]{:S(2)}) copy-start(f32[1,2048]{1,0:T(1,128)} %get-tuple-element.114) | copy-start | bytes 24580
  352.3 111.0 %copy-start.1 = (f32[8,1088]{1,0:T(8,128)S(1)}, f32[8,1088]{1,0:T(8,128)}, u32[]{:S(2)}) copy-start(f32[8,1088]{1,0:T(8,128)} %get-tuple-element.113) | copy-start | bytes 104452
  352.3 111.0 %copy-start.2 = (f32[1,2304]{1,0:T(1,128)S(1)}, f32[1,2304]{1,0:T(1,128)}, u32[]{:S(2)}) copy-start(f32[1,2304]{1,0:T(1,128)} %get-tuple-element.115) | copy-start | bytes 27652
